TPU v7x, 32 devices: a whole 2x2x4 slice. The times are simulated.
32 devices in a mesh: seg: 4 (over x, core), seq: 8 (over z, y).
Axes of the slice: x: 2, y: 2, z: 4, core: 2. Of those that a mesh axis runs over, the one named last changes fastest.
Arguments:
- queries: bfloat16 [4096, 4096], P(('seg', 'seq')), may hold values from -6 to 6
- keys: bfloat16 [4096, 4096], P(('seg', 'seq')), may hold values from -6 to 6
- values: bfloat16 [4096, 4096], P(('seg', 'seq')), may hold values from -6 to 6
- prior_keys: bfloat16 [1024, 4096], P('seq'), may hold values from -6 to 6
- prior_values: bfloat16 [1024, 4096], P('seq'), may hold values from -6 to 6
- conv_keys: bfloat16 [32, 512, 128], P('seq'), may hold values from -0.5 to 0.5
- conv_values: bfloat16 [32, 512, 128], P('seq'), may hold values from -0.5 to 0.5
- doc_starts: int32 [4], replicated, may hold values from 0 to 2047, as said below
Outputs:
- attended: bfloat16 [4096, 4096], P(('seg', 'seq'))
- compressed_keys: bfloat16 [1024, 4096], P('seg', 'seq')
- compressed_values: bfloat16 [1024, 4096], P('seg', 'seq')
- recon_loss: float32 [], replicated
- grad_conv_keys: float32 [32, 512, 128], P('seq')
- grad_conv_values: float32 [32, 512, 128], P('seq')
Inputs may be any that keep to these rules, and one draw needn't show every extreme that they name: `doc_starts`: entry g is the offset within segment g at which a document starts; an entry of 1024 or more means segment g continues the document before it. Entry 0 is 2047, entries 1 and 2 are 1024 or more, entry 3 lies from 512 to 1023.
All inputs are finite; a program needn't handle non-finite values.
Results may differ from a plain program's by a relative error of at most 0.015.
Values may be sent and summed in bfloat16 or wider, within the bound.
No kernel may reach another device: no remote copies, remote signals or barrier semaphores. Data moves between devices by JAX's collectives and lax.ppermute only.
A program may use at most 64 MiB of HBM per device.

v0:
```python
import math

import jax
import jax.numpy as jnp
from jax import lax
from jax.sharding import PartitionSpec as P

RATE = 4


def shifted_2(block, axis, distance):
    devices = range(lax.axis_size(axis))
    route = [(i - distance, i) for i in devices if i - distance in devices]
    return lax.ppermute(block, axis, route)


def pick_entry(small_table, wanted):
    return jnp.sum(jnp.where(jnp.arange(small_table.shape[0]) == wanted, small_table, 0))


def compress(source_rows, weight):
    head_count = weight.shape[0]
    head_width = weight.shape[2]
    windows = source_rows.reshape(source_rows.shape[0] // RATE, RATE, head_count, head_width)
    kernel = weight.reshape(head_count, RATE, head_width, head_width)
    merged = jnp.einsum("crhd,hrde->che", windows, kernel, preferred_element_type=jnp.float32)
    return merged.reshape(merged.shape[0], head_count * head_width).astype(jnp.bfloat16)


def on_device(queries, keys, values, prior_keys, prior_values, conv_keys, conv_values, doc_starts):
    seq_count = lax.axis_size("seq")
    seg_count = lax.axis_size("seg")
    group_index = lax.axis_index("seg")
    seg_rows = queries.shape[0] * seq_count
    head_count = conv_keys.shape[0]
    head_width = conv_keys.shape[2]
    comp_rows = seg_rows // RATE
    score_scale = 1.0 / math.sqrt(head_width)
    first_group = group_index == 0
    shifted = shifted_2(jnp.stack((keys, values)), "seg", 1)
    previous = jnp.where(first_group, jnp.stack((prior_keys, prior_values)), shifted)
    moved = (
        lax.all_to_all(queries, "seq", split_axis=1, concat_axis=0, tiled=True),
        lax.all_to_all(keys, "seq", split_axis=1, concat_axis=0, tiled=True),
        lax.all_to_all(values, "seq", split_axis=1, concat_axis=0, tiled=True),
        lax.all_to_all(previous[0], "seq", split_axis=1, concat_axis=0, tiled=True),
        lax.all_to_all(previous[1], "seq", split_axis=1, concat_axis=0, tiled=True),
    )
    query_heads = moved[0]
    key_heads = moved[1]
    value_heads = moved[2]
    fine_keys = moved[3]
    fine_values = moved[4]
    comp_keys = compress(fine_keys, conv_keys)
    comp_values = compress(fine_values, conv_values)
    memory = shifted_2(jnp.stack((comp_keys, comp_values)), "seg", 1)
    start_now = pick_entry(doc_starts, group_index)
    start_prev = jnp.where(group_index >= 1, pick_entry(doc_starts, group_index - 1), seg_rows)
    start_back = jnp.where(group_index >= 2, pick_entry(doc_starts, group_index - 2), seg_rows)
    lead_prev = jnp.where(start_prev < seg_rows, start_prev, 0)
    lead_back = jnp.where(start_back < seg_rows, start_back, 0)
    comp_open = (group_index >= 1) & (start_prev >= seg_rows)
    all_keys = jnp.concatenate((memory[0], fine_keys, key_heads), axis=0)
    all_values = jnp.concatenate((memory[1], fine_values, value_heads), axis=0)
    block_rows = math.gcd(seg_rows, 512)
    block_count = seg_rows // block_rows
    column = jnp.arange(comp_rows + 2 * seg_rows, dtype=jnp.int32)[None, :]
    comp_part = column < comp_rows
    fine_part = (column >= comp_rows) & (column < comp_rows + seg_rows)
    own_part = column >= comp_rows + seg_rows
    key_place = jnp.where(
        comp_part,
        RATE * column,
        jnp.where(fine_part, column - comp_rows, column - comp_rows - seg_rows),
    )

    def attend_block(flat_index):
        head_index = flat_index // block_count
        block_index = flat_index % block_count
        query_block = lax.dynamic_slice(
            query_heads,
            (block_index * block_rows, head_index * head_width),
            (block_rows, head_width),
        )
        key_block = lax.dynamic_slice_in_dim(all_keys, head_index * head_width, head_width, 1)
        value_block = lax.dynamic_slice_in_dim(all_values, head_index * head_width, head_width, 1)
        scores = (
            jnp.einsum("qd,kd->qk", query_block, key_block, preferred_element_type=jnp.float32)
            * score_scale
        )
        query_place = block_index * block_rows + jnp.arange(block_rows, dtype=jnp.int32)[:, None]
        before_doc = query_place < start_now
        seen_comp = comp_part & comp_open & before_doc & (key_place >= lead_back)
        seen_fine = fine_part & before_doc & (key_place >= lead_prev)
        seen_own = own_part & (key_place <= query_place) & ((key_place >= start_now) | before_doc)
        visible = seen_comp | seen_fine | seen_own
        row_top = jnp.max(jnp.where(visible, scores, -jnp.inf), axis=1, keepdims=True)
        weights = jnp.exp(jnp.where(visible, scores - row_top, -jnp.inf))
        row_total = jnp.sum(weights, axis=1, keepdims=True)
        mixed_rows = (
            jnp.dot(weights.astype(jnp.bfloat16), value_block, preferred_element_type=jnp.float32)
            / row_total
        )
        return mixed_rows.astype(jnp.bfloat16)

    pieces = lax.map(attend_block, jnp.arange(head_count * block_count, dtype=jnp.int32))
    attended_heads = (
        pieces.reshape(head_count, seg_rows, head_width)
        .transpose(1, 0, 2)
        .reshape(seg_rows, head_count * head_width)
    )
    attended = lax.all_to_all(attended_heads, "seq", split_axis=0, concat_axis=1, tiled=True)

    def recon_head(head_index):
        start_col = head_index * head_width
        query_full = lax.dynamic_slice_in_dim(query_heads, start_col, head_width, 1)
        fine_k = lax.dynamic_slice_in_dim(fine_keys, start_col, head_width, 1)
        fine_v = lax.dynamic_slice_in_dim(fine_values, start_col, head_width, 1)
        comp_k = lax.dynamic_slice_in_dim(comp_keys, start_col, head_width, 1)
        comp_v = lax.dynamic_slice_in_dim(comp_values, start_col, head_width, 1)

        def recon_step(running, block_index):
            loss_sum, value_acc, key_acc = running
            query_block = lax.dynamic_slice_in_dim(
                query_full, block_index * block_rows, block_rows, 0
            )
            fine_scores = (
                jnp.einsum("qd,kd->qk", query_block, fine_k, preferred_element_type=jnp.float32)
                * score_scale
            )
            fine_exp = jnp.exp(fine_scores - jnp.max(fine_scores, axis=1, keepdims=True))
            fine_total = jnp.sum(fine_exp, axis=1, keepdims=True)
            recon_fine = (
                jnp.dot(fine_exp.astype(jnp.bfloat16), fine_v, preferred_element_type=jnp.float32)
                / fine_total
            )
            comp_scores = (
                jnp.einsum("qd,kd->qk", query_block, comp_k, preferred_element_type=jnp.float32)
                * score_scale
            )
            comp_exp = jnp.exp(comp_scores - jnp.max(comp_scores, axis=1, keepdims=True))
            comp_total = jnp.sum(comp_exp, axis=1, keepdims=True)
            comp_weights = comp_exp.astype(jnp.bfloat16)
            recon_comp = (
                jnp.dot(comp_weights, comp_v, preferred_element_type=jnp.float32) / comp_total
            )
            differ = recon_fine - recon_comp
            out_grad = (-2.0 * differ / comp_total).astype(jnp.bfloat16)
            value_acc = value_acc + jnp.einsum(
                "qc,qd->cd", comp_weights, out_grad, preferred_element_type=jnp.float32
            )
            inner_grad = jnp.einsum(
                "qd,cd->qc", out_grad, comp_v, preferred_element_type=jnp.float32
            )
            row_offset = jnp.sum(out_grad.astype(jnp.float32) * recon_comp, axis=1, keepdims=True)
            score_grad = (comp_exp * (inner_grad - row_offset)).astype(jnp.bfloat16)
            key_acc = key_acc + jnp.einsum(
                "qc,qd->cd", score_grad, query_block, preferred_element_type=jnp.float32
            )
            return ((loss_sum + jnp.sum(differ * differ), value_acc, key_acc), None)

        zero_rows = jnp.zeros((comp_rows, head_width), jnp.float32)
        start_state = (jnp.zeros((), jnp.float32), zero_rows, zero_rows)
        (loss_sum, value_acc, key_acc), unused = lax.scan(
            recon_step, start_state, jnp.arange(block_count, dtype=jnp.int32)
        )
        key_grad = (key_acc * score_scale).astype(jnp.bfloat16)
        value_grad = value_acc.astype(jnp.bfloat16)
        windows_k = fine_k.reshape(comp_rows, RATE * head_width)
        windows_v = fine_v.reshape(comp_rows, RATE * head_width)
        grad_k = jnp.einsum("cw,cd->wd", windows_k, key_grad, preferred_element_type=jnp.float32)
        grad_v = jnp.einsum("cw,cd->wd", windows_v, value_grad, preferred_element_type=jnp.float32)
        return (loss_sum, grad_k, grad_v)

    losses, grad_k, grad_v = lax.map(recon_head, jnp.arange(head_count, dtype=jnp.int32))
    grad_k, grad_v = (
        lax.psum(grad_k.astype(jnp.bfloat16), "seg").astype(jnp.float32),
        lax.psum(grad_v.astype(jnp.bfloat16), "seg").astype(jnp.float32),
    )
    total_loss = lax.psum(jnp.sum(losses), ("seg", "seq"))
    recon_loss = total_loss / (seg_count * seg_rows)
    return (attended, comp_keys, comp_values, recon_loss, grad_k, grad_v)


def solution(mesh):
    return jax.shard_map(
        on_device,
        mesh=mesh,
        in_specs=(
            P(("seg", "seq"), None),
            P(("seg", "seq"), None),
            P(("seg", "seq"), None),
            P("seq", None),
            P("seq", None),
            P("seq", None, None),
            P("seq", None, None),
            P(),
        ),
        out_specs=(
            P(("seg", "seq"), None),
            P("seg", "seq"),
            P("seg", "seq"),
            P(),
            P("seq", None, None),
            P("seq", None, None),
        ),
        check_vma=False,
    )
```

profile of v0, /device:TPU:0, one launch (start us, length us, event | category | flops | bytes accessed | tf_op | source)
XLA Modules:
  0.0 430.9 jit_solution(13508023119754773481)
XLA Ops:
  7.2 3.2 pad_maximum_fusion.2
  10.4 3.6 collective-permute-start
  15.1 6.7 %all-to-all-start.4 = ((bf16[128,8,512]{2,0,1:T(8,128)(2,1)}), bf16[128,8,512]{2,0,1:T(8,128)(2,1)S(1)}, u32[]{:S(2)}, u32[]{:S(2)}) async-start(bf16[128,8,512]{2,0,1:T(8,128)(2,1)} %bitcast.97), calls=%async_computation.4 | async-start | bytes 2097152 | tf_op jit(solution)/shard_map/all_to_all | solution.py:45
  25.2 23.0 %all-to-all-done.4 = bf16[128,8,512]{2,0,1:T(8,128)(2,1)S(1)} async-done(((bf16[128,8,512]{2,0,1:T(8,128)(2,1)}), bf16[128,8,512]{2,0,1:T(8,128)(2,1)S(1)}, u32[]{:S(2)}, u32[]{:S(2)}) %all-to-all-start.4) | async-done | bytes 1048608 | tf_op jit(solution)/shard_map/all_to_all | solution.py:45
  48.2 4.2 all-to-all-start.1
  54.2 24.0 %all-to-all-done.1 = bf16[128,8,512]{2,0,1:T(8,128)(2,1)} async-done(((bf16[128,8,512]{2,0,1:T(8,128)(2,1)}), bf16[128,8,512]{2,0,1:T(8,128)(2,1)}, u32[]{:S(2)}, u32[]{:S(2)}) %all-to-all-start.1) | async-done | bytes 1048608 | tf_op jit(solution)/shard_map/all_to_all | solution.py:46
  78.1 3.6 all-to-all-start.2
  82.8 24.8 %all-to-all-done.2 = bf16[128,8,512]{2,0,1:T(8,128)(2,1)S(1)} async-done(((bf16[128,8,512]{2,0,1:T(8,128)(2,1)}), bf16[128,8,512]{2,0,1:T(8,128)(2,1)S(1)}, u32[]{:S(2)}, u32[]{:S(2)}) %all-to-all-start.2) | async-done | bytes 1048608 | tf_op jit(solution)/shard_map/all_to_all | solution.py:47
  107.6 3.6 all-to-all-start.3
  111.2 2.3 copy.101
  114.6 2.2 reshape.199
  118.5 18.6 %all-to-all-done.3 = bf16[128,8,512]{2,0,1:T(8,128)(2,1)S(1)} async-done(((bf16[128,8,512]{2,0,1:T(8,128)(2,1)}), bf16[128,8,512]{2,0,1:T(8,128)(2,1)S(1)}, u32[]{:S(2)}, u32[]{:S(2)}) %all-to-all-start.3) | async-done | bytes 1048608 | tf_op jit(solution)/shard_map/all_to_all | solution.py:44
  137.2 4.2 all-to-all-start
  154.6 2.9 pad_maximum_fusion
  157.5 9.6 %all-to-all-done = bf16[128,8,512]{2,0,1:T(8,128)(2,1)} async-done(((bf16[128,8,512]{2,0,1:T(8,128)(2,1)}), bf16[128,8,512]{2,0,1:T(8,128)(2,1)}, u32[]{:S(2)}, u32[]{:S(2)}) %all-to-all-start) | async-done | bytes 1048608 | tf_op jit(solution)/shard_map/all_to_all | solution.py:43
  167.1 130.6 %while.45 = (s32[]{:T(128)}, bf16[8,512,128]{2,1,0:T(8,128)(2,1)S(1)}, pred[]{:T(512)}, s32[8]{0:T(128)S(1)}, s32[]{:T(128)}, /*index=5*/s32[]{:T(128)}, s32[]{:...) while((s32[]{:T(128)}, ...), condition=%wide.region_6.7_spmd.clone.clone, body=%wide.region_3.6_spmd.clone.clone.sunk | while | flops 650159104 | bytes 15729129 | solution.py:106
  171.8 3.7 select_reduce_fusion.2
  175.5 3.9 fusion.118
  179.5 3.9 fusion.119
  188.1 3.7 select_reduce_fusion.2
  191.8 3.9 fusion.118
  195.8 3.9 fusion.119
  204.4 3.7 select_reduce_fusion.2
  208.2 3.9 fusion.118
  212.1 3.9 fusion.119
  220.8 3.7 select_reduce_fusion.2
  224.5 3.9 fusion.118
  228.4 3.9 fusion.119
  237.1 3.7 select_reduce_fusion.2
  240.8 3.9 fusion.118
  244.8 3.9 fusion.119
  253.4 3.7 select_reduce_fusion.2
  257.1 3.9 fusion.118
  261.1 3.9 fusion.119
  269.7 3.7 select_reduce_fusion.2
  273.5 3.9 fusion.118
  277.4 3.9 fusion.119
  286.0 3.7 select_reduce_fusion.2
  289.8 3.9 fusion.118
  293.7 3.9 fusion.119
  301.5 4.2 all-to-all-start.5
  306.0 69.4 %while.44 = (s32[]{:T(128)}, f32[4]{0:T(128)S(1)}, bf16[4,512,128]{2,1,0:T(8,128)(2,1)}, bf16[4,512,128]{2,1,0:T(8,128)(2,1)}, s32[4]{0:T(128)S(1)}, /*index=5*/...) while((s32[]{:T(128)}, f32[4]{0:T(128)S(1)}, ...), condition=%wide.region_16.17_spmd, body=%wide.region_7.16_spmd.sunk | while | flops 510031360 | bytes 15694469 | solution.py:175
  310.2 10.9 %while.46 = (s32[]{:T(128)}, f32[]{:T(128)}, f32[256,128]{1,0:T(8,128)S(1)}, f32[256,128]{1,0:T(8,128)S(1)}, s32[2]{0:T(128)S(1)}, /*index=5*/bf16[1024,128]{1,0...) while((s32[]{:T(128)}, f32[]{:T(128)}, ...), condition=%wide.region_15.15_spmd.clone, body=%wide.region_8.14_spmd.clone.sunk | while | flops 442824192 | bytes 11499758 | solution.py:164
  327.5 10.9 %while.46 = (s32[]{:T(128)}, f32[]{:T(128)}, f32[256,128]{1,0:T(8,128)S(1)}, f32[256,128]{1,0:T(8,128)S(1)}, s32[2]{0:T(128)S(1)}, /*index=5*/bf16[1024,128]{1,0...) while((s32[]{:T(128)}, f32[]{:T(128)}, ...), condition=%wide.region_15.15_spmd.clone, body=%wide.region_8.14_spmd.clone.sunk | while | flops 442824192 | bytes 11499758 | solution.py:164
  344.9 10.9 %while.46 = (s32[]{:T(128)}, f32[]{:T(128)}, f32[256,128]{1,0:T(8,128)S(1)}, f32[256,128]{1,0:T(8,128)S(1)}, s32[2]{0:T(128)S(1)}, /*index=5*/bf16[1024,128]{1,0...) while((s32[]{:T(128)}, f32[]{:T(128)}, ...), condition=%wide.region_15.15_spmd.clone, body=%wide.region_8.14_spmd.clone.sunk | while | flops 442824192 | bytes 11499758 | solution.py:164
  362.2 10.9 %while.46 = (s32[]{:T(128)}, f32[]{:T(128)}, f32[256,128]{1,0:T(8,128)S(1)}, f32[256,128]{1,0:T(8,128)S(1)}, s32[2]{0:T(128)S(1)}, /*index=5*/bf16[1024,128]{1,0...) while((s32[]{:T(128)}, f32[]{:T(128)}, ...), condition=%wide.region_15.15_spmd.clone, body=%wide.region_8.14_spmd.clone.sunk | while | flops 442824192 | bytes 11499758 | solution.py:164
  376.0 39.8 %psum.21 = f32[]{:T(128)} all-reduce(f32[]{:T(128)} %reduce_sum.87), channel_id=1, replica_groups=mesh['seg'=4,'seq'=8] {'seg','seq'}, use_global_device_ids=true, to_apply=%region_18.19 | all-reduce | flops 1 | bytes 8 | tf_op jit(solution)/shard_map/psum | solution.py:180
  420.7 2.3 copy.78
  (244 shorter events, 102.9 us)
Async XLA Ops:
  7.2 109.7 %copy-start = (bf16[4,512,128]{2,1,0:T(8,128)(2,1)S(1)}, bf16[4,512,128]{2,1,0:T(8,128)(2,1)}, u32[]{:S(2)}) copy-start(bf16[4,512,128]{2,1,0:T(8,128)(2,1)} %param.20) | copy-start | bytes 1572868
  7.2 6.9 %copy-start.1 = (bf16[128,4096]{1,0:T(8,128)(2,1)S(1)}, bf16[128,4096]{1,0:T(8,128)(2,1)}, u32[]{:S(2)}) copy-start(bf16[128,4096]{1,0:T(8,128)(2,1)} %param.16) | copy-start | bytes 3145732
  10.4 11.4 %collective-permute-start = (bf16[2,128,4096]{2,1,0:T(8,128)(2,1)}, bf16[2,128,4096]{2,1,0:T(8,128)(2,1)}, u32[]{:S(2)}, u32[]{:S(2)}) collective-permute-start(bf16[2,128,4096]{2,1,0:T(8,128)(2,1)} %pad_maximum_fusion.2), channel_id=1, source_target_pairs={{0,8},{8,16},{16,24},{1,9},{9,17},{17,25},{2,10},{10,18},{18,26},{... | collective-permute-start | bytes 6291464 | tf_op jit(solution)/shard_map/ppermute | solution.py:14
  14.0 7.7 %copy-start.7 = (bf16[128,4096]{1,0:T(8,128)(2,1)S(1)}, bf16[128,4096]{1,0:T(8,128)(2,1)}, u32[]{:S(2)}) copy-start(bf16[128,4096]{1,0:T(8,128)(2,1)} %param.18) | copy-start | bytes 3145732
  15.1 33.1 %all-to-all-start.4 = ((bf16[128,8,512]{2,0,1:T(8,128)(2,1)}), bf16[128,8,512]{2,0,1:T(8,128)(2,1)S(1)}, u32[]{:S(2)}, u32[]{:S(2)}) async-start(bf16[128,8,512]{2,0,1:T(8,128)(2,1)} %bitcast.97), calls=%async_computation.4 | async-start | bytes 2097152 | tf_op jit(solution)/shard_map/all_to_all | solution.py:45
  48.2 4.7 %copy-start.3 = (bf16[128,8,512]{2,0,1:T(8,128)(2,1)}, bf16[128,8,512]{2,0,1:T(8,128)(2,1)S(1)}, u32[]{:S(2)}) copy-start(bf16[128,8,512]{2,0,1:T(8,128)(2,1)S(1)} %all-to-all-done.4) | copy-start | bytes 3145732
  48.2 29.9 %all-to-all-start.1 = ((bf16[128,8,512]{2,0,1:T(8,128)(2,1)}), bf16[128,8,512]{2,0,1:T(8,128)(2,1)}, u32[]{:S(2)}, u32[]{:S(2)}) async-start(bf16[128,8,512]{2,0,1:T(8,128)(2,1)} %copy.64), calls=%async_computation.1 | async-start | bytes 2097152 | tf_op jit(solution)/shard_map/all_to_all | solution.py:46
  52.9 28.8 %copy-start.2 = (bf16[128,4096]{1,0:T(8,128)(2,1)S(1)}, bf16[128,4096]{1,0:T(8,128)(2,1)}, u32[]{:S(2)}) copy-start(bf16[128,4096]{1,0:T(8,128)(2,1)} %param.15) | copy-start | bytes 3145732
  78.1 29.5 %all-to-all-start.2 = ((bf16[128,8,512]{2,0,1:T(8,128)(2,1)}), bf16[128,8,512]{2,0,1:T(8,128)(2,1)S(1)}, u32[]{:S(2)}, u32[]{:S(2)}) async-start(bf16[128,8,512]{2,0,1:T(8,128)(2,1)} %copy.67), calls=%async_computation.2 | async-start | bytes 2097152 | tf_op jit(solution)/shard_map/all_to_all | solution.py:47
  107.6 29.6 %all-to-all-start.3 = ((bf16[128,8,512]{2,0,1:T(8,128)(2,1)}), bf16[128,8,512]{2,0,1:T(8,128)(2,1)S(1)}, u32[]{:S(2)}, u32[]{:S(2)}) async-start(bf16[128,8,512]{2,0,1:T(8,128)(2,1)} %bitcast.98), calls=%async_computation.3 | async-start | bytes 2097152 | tf_op jit(solution)/shard_map/all_to_all | solution.py:44
  137.2 6.1 %copy-start.5 = (bf16[128,8,512]{2,0,1:T(8,128)(2,1)}, bf16[128,8,512]{2,0,1:T(8,128)(2,1)S(1)}, u32[]{:S(2)}) copy-start(bf16[128,8,512]{2,0,1:T(8,128)(2,1)S(1)} %all-to-all-done.3) | copy-start | bytes 3145732
  137.2 29.9 %all-to-all-start = ((bf16[128,8,512]{2,0,1:T(8,128)(2,1)}), bf16[128,8,512]{2,0,1:T(8,128)(2,1)}, u32[]{:S(2)}, u32[]{:S(2)}) async-start(bf16[128,8,512]{2,0,1:T(8,128)(2,1)} %bitcast.99), calls=%async_computation | async-start | bytes 2097152 | tf_op jit(solution)/shard_map/all_to_all | solution.py:43
  141.4 6.8 %copy-start.10 = (s32[4]{0:T(128)S(1)}, s32[4]{0:T(128)}, u32[]{:S(2)}) copy-start(s32[4]{0:T(128)} %param.21) | copy-start | bytes 52
  143.3 9.7 %copy-start.4 = (bf16[128,8,512]{2,0,1:T(8,128)(2,1)S(1)}, bf16[128,8,512]{2,0,1:T(8,128)(2,1)}, u32[]{:S(2)}) copy-start(bf16[128,8,512]{2,0,1:T(8,128)(2,1)} %copy-done.3) | copy-start | bytes 3145732
  146.1 5.8 %collective-permute-start.1 = (bf16[2,256,512]{2,1,0:T(8,128)(2,1)}, bf16[2,256,512]{2,1,0:T(8,128)(2,1)}, u32[]{:S(2)}, u32[]{:S(2)}) collective-permute-start(bf16[2,256,512]{2,1,0:T(8,128)(2,1)} %pad_maximum_fusion.3), channel_id=1, source_target_pairs={{0,8},{8,16},{16,24},{1,9},{9,17},{17,25},{2,10},{10,18},{18,26},{... | collective-permute-start | bytes 1572872 | tf_op jit(solution)/shard_map/ppermute | solution.py:14
  153.1 1.6 copy-start.6
  154.6 12.5 %copy-start.8 = (bf16[8,512,128]{2,1,0:T(8,128)(2,1)S(1)}, bf16[8,512,128]{2,1,0:T(8,128)(2,1)}, u32[]{:S(2)}) copy-start(bf16[8,512,128]{2,1,0:T(8,128)(2,1)} %custom-call.5) | copy-start | bytes 3145732
  297.6 1.0 copy-start.9
  301.5 119.2 %all-to-all-start.5 = ((bf16[8,128,512]{1,2,0:T(8,128)(2,1)}), bf16[8,128,512]{1,2,0:T(8,128)(2,1)}, u32[]{:S(2)}, u32[]{:S(2)}) async-start(bf16[8,128,512]{1,2,0:T(8,128)(2,1)} %copy.75), calls=%async_computation.5 | async-start | bytes 2097152 | tf_op jit(solution)/shard_map/all_to_all | solution.py:112
  305.8 110.8 %all-reduce.3.cloned.1.call-start = ((), (), s32[]{:S(2)}) async-start(), calls=%async_computation.6 | async-start | bytes 2097152 | tf_op jit(solution)/shard_map/psum | solution.py:177
Sparse Core Ops, SparseCore 0:
  375.6 36.5 all-reduce.2
where the time goes:
time: 434 us; the launch traced here: 431 us
  waiting for transfers between devices  100 us (23%)
  matrix products  95.1 us (22%)
  other arithmetic  64.7 us (15%)
  local copies, waits for them, and re-layouts  46.2 us (11%)
  blocking collectives  39.8 us (9%)
  loops' own time  35 us (8%)
  starting transfers between devices  32.6 us (8%)
  between operations  17.4 us (4%)
    psum x1, blocking collectives, on_device(): total_loss = lax.psum(jnp.sum(losses), ('seg', 'seq'))  39.8 us
    reduce_sum x8, other arithmetic, attend_block(): row_total = jnp.sum(weights, axis=1, keepdims=True)  31.6 us
    dot_general x8, matrix products, attend_block(): jnp.dot(weights.astype(jnp.bfloat16), value_block, preferred_element_type...  31.3 us
    dot_general x8, matrix products, attend_block(): jnp.einsum('qd,kd->qk', query_block, key_block, preferred_element_type=jn...  29.9 us
    all_to_all x1, waiting for transfers between devices, on_device(): lax.all_to_all(previous[1], 'seq', split_axis=1, concat_axis=0, tiled=True)  24.8 us
    all_to_all x1, waiting for transfers between devices, on_device(): lax.all_to_all(previous[0], 'seq', split_axis=1, concat_axis=0, tiled=True)  24 us
    all_to_all x1, waiting for transfers between devices, on_device(): lax.all_to_all(values, 'seq', split_axis=1, concat_axis=0, tiled=True)  23 us
    another operation x1, loops' own time, on_device(): lax.map(attend_block, jnp.arange(head_count * block_count, dtype=jnp.int32))  21.3 us
  transfers between devices with their start and end apart: 9, of which 5 were waited for; matrix products, arithmetic and copies ran while one was open for 20% of the time, Pallas kernels for 0%

commit v1 on v0

--- a/solution.py
+++ b/solution.py
@@ -1,11 +1,417 @@
+import functools
 import math
 
 import jax
 import jax.numpy as jnp
 from jax import lax
+from jax.experimental import pallas as pl
+from jax.experimental.pallas import tpu as pltpu
 from jax.sharding import PartitionSpec as P
 
 RATE = 4
+HIDDEN = -1e30
+BOTH = ("seg", "seq")
+
+
+def on_vmem(limit_mib=60):
+    return pltpu.CompilerParams(vmem_limit_bytes=limit_mib * 2**20)
+
+
+def pack_kernel(rows, share, where_ref, q_ref, k_ref, v_ref, pk_ref, pv_ref, out_ref):
+    del where_ref
+    width = out_ref.shape[-1]
+    for r in range(out_ref.shape[0]):
+        columns = slice(r * width, (r + 1) * width)
+        out_ref[r, 0, 0:rows, :] = q_ref[:, columns]
+        out_ref[r, 0, rows : 2 * rows, :] = k_ref[:, columns]
+        out_ref[r, 0, 2 * rows : 3 * rows, :] = v_ref[:, columns]
+        out_ref[r, 0, 3 * rows : 3 * rows + share, :] = pk_ref[:, columns]
+        out_ref[r, 0, 3 * rows + share :, :] = pv_ref[:, columns]
+
+
+def pack(seg_at, queries, keys, values, prior_keys, prior_values, seg_count, seq_count):
+    rows, columns = queries.shape
+    share = rows // seg_count
+    block = 3 * rows + 2 * share
+    wide = columns // seq_count
+    width = wide // seg_count
+    whole = pl.BlockSpec((rows, wide), lambda s, at: (0, s))
+    part = pl.BlockSpec((share, wide), lambda s, at: (at[0], s))
+    return pl.pallas_call(
+        functools.partial(pack_kernel, rows, share),
+        out_shape=jax.ShapeDtypeStruct((seg_count, seq_count, block, width), queries.dtype),
+        grid_spec=pltpu.PrefetchScalarGridSpec(
+            num_scalar_prefetch=1,
+            grid=(seq_count,),
+            in_specs=[whole, whole, whole, part, part],
+            out_specs=pl.BlockSpec((seg_count, 1, block, width), lambda s, at: (0, s, 0, 0)),
+        ),
+        compiler_params=on_vmem(),
+        name="pack",
+    )(seg_at, queries, keys, values, prior_keys, prior_values)
+
+
+def unpack_kernel(in_ref, out_ref):
+    width = in_ref.shape[-1]
+    for r in range(in_ref.shape[0]):
+        out_ref[:, r * width : (r + 1) * width] = in_ref[r, 0]
+
+
+def unpack(blocks):
+    seg_count, seq_count, rows, width = blocks.shape
+    return pl.pallas_call(
+        unpack_kernel,
+        out_shape=jax.ShapeDtypeStruct((rows, seg_count * seq_count * width), blocks.dtype),
+        grid=(seq_count,),
+        in_specs=[pl.BlockSpec((seg_count, 1, rows, width), lambda s: (0, s, 0, 0))],
+        out_specs=pl.BlockSpec((rows, seg_count * width), lambda s: (0, s)),
+        compiler_params=on_vmem(),
+        name="unpack",
+    )(blocks)
+
+
+def matmul_t(a, b):
+    return lax.dot_general(a, b, (((1,), (1,)), ((), ())), preferred_element_type=jnp.float32)
+
+
+def t_matmul(a, b):
+    return lax.dot_general(a, b, (((0,), (0,)), ((), ())), preferred_element_type=jnp.float32)
+
+
+def matmul(a, b):
+    return jnp.dot(a, b, preferred_element_type=jnp.float32)
+
+
+def mixed(scores, rate, values_and_ones):
+    top = jnp.max(scores, axis=1, keepdims=True)
+    weights = jnp.exp2((scores - top) * rate).astype(jnp.bfloat16)
+    return top, matmul(weights, values_and_ones)
+
+
+def attend_kernel(
+    dims,
+    starts_ref, at_ref, recv_ref, prior_ref, conv_k_ref, conv_v_ref,
+    out_ref, recon_ref, comp_k_ref, comp_v_ref, win_k_ref, win_v_ref,
+    fine_k, fine_v, cat_k, cat_v, rows_f32,
+):
+    rows, share, seg_count, seq_count, step = dims
+    g = pl.program_id(0)
+    seg_rows = rows * seq_count
+    comp_rows = seg_rows // RATE
+    width = recv_ref.shape[-1]
+    rate = math.log2(math.e) / math.sqrt(width)
+    bf16 = jnp.bfloat16
+
+    @pl.when(g == 0)
+    def _():
+        cat_k[0:comp_rows, :] = jnp.zeros((comp_rows, width), bf16)
+        cat_v[0:comp_rows, 0:width] = jnp.zeros((comp_rows, width), bf16)
+        cat_v[:, width:] = jnp.ones((comp_rows + seg_rows, width), bf16)
+        fine_v[:, width:] = jnp.ones((seg_rows, width), bf16)
+        for s in range(seq_count):
+            for i in range(seg_count):
+                at = s * rows + i * share
+                fine_k[at : at + share, :] = prior_ref[i, s, 0:share, :]
+                fine_v[at : at + share, 0:width] = prior_ref[i, s, share:, :]
+
+    @pl.when(g > 0)
+    def _():
+        fine_k[...] = cat_k[comp_rows:, :]
+        fine_v[:, 0:width] = cat_v[comp_rows:, 0:width]
+
+    own_k = recv_ref[0, :, rows : 2 * rows, :].reshape(seg_rows, width)
+    own_v = recv_ref[0, :, 2 * rows : 3 * rows, :].reshape(seg_rows, width)
+    cat_k[comp_rows:, :] = own_k
+    cat_v[comp_rows:, 0:width] = own_v
+
+    for fine, conv, comp, win in (
+        (fine_k, conv_k_ref, comp_k_ref, win_k_ref),
+        (fine_v, conv_v_ref, comp_v_ref, win_v_ref),
+    ):
+        rows_f32[...] = fine[:, 0:width].astype(jnp.float32)
+        for r in range(RATE):
+            win[0, :, r * width : (r + 1) * width] = rows_f32[
+                pl.ds(r, comp_rows, stride=RATE), :
+            ].astype(bf16)
+        comp[0] = matmul(win[0], conv[0]).astype(bf16)
+
+    def start_of(i):
+        return jnp.where(i >= 0, starts_ref[jnp.maximum(i, 0)], seg_rows)
+
+    b0, b1, b2 = start_of(g), start_of(g - 1), start_of(g - 2)
+    s1 = jnp.where(b1 < seg_rows, b1, 0)
+    s2 = jnp.where(b2 < seg_rows, b2, 0)
+    memory_from = jnp.where((g >= 1) & (b1 >= seg_rows), s2, RATE * comp_rows)
+
+    def attend(doc, fine_from_s1):
+        for p0 in range(0, seg_rows, step):
+            blocks = slice(p0 // rows, (p0 + step) // rows)
+            q = recv_ref[0, blocks, 0:rows, :].reshape(step, width)
+            fine_scores = matmul_t(q, fine_k[...])
+            fine_top, fine_mix = mixed(fine_scores, rate, fine_v[...])
+            recon_ref[p0 : p0 + step, :] = fine_mix[:, 0:width] / fine_mix[:, width:]
+            if fine_from_s1:
+                place = lax.broadcasted_iota(jnp.int32, (step, seg_rows), 1)
+                fine_top, fine_mix = mixed(
+                    jnp.where(place >= s1, fine_scores, HIDDEN), rate, fine_v[...]
+                )
+
+            seen = comp_rows + p0 + step
+            scores = matmul_t(q, cat_k[0:seen, :])
+            place_q = p0 + lax.broadcasted_iota(jnp.int32, (step, comp_rows), 0)
+            place_k = RATE * lax.broadcasted_iota(jnp.int32, (step, comp_rows), 1)
+            memory_seen = place_k >= memory_from
+            if doc:
+                memory_seen &= place_q < b0
+            parts = [jnp.where(memory_seen, scores[:, 0:comp_rows], HIDDEN)]
+            if doc:
+                place_q = p0 + lax.broadcasted_iota(jnp.int32, (step, p0 + step), 0)
+                place_k = lax.broadcasted_iota(jnp.int32, (step, p0 + step), 1)
+                own_seen = (place_k <= place_q) & ((place_k >= b0) | (place_q < b0))
+                parts.append(jnp.where(own_seen, scores[:, comp_rows:], HIDDEN))
+            else:
+                if p0:
+                    parts.append(scores[:, comp_rows : comp_rows + p0])
+                place_q = lax.broadcasted_iota(jnp.int32, (step, step), 0)
+                place_k = lax.broadcasted_iota(jnp.int32, (step, step), 1)
+                parts.append(jnp.where(place_k <= place_q, scores[:, comp_rows + p0 :], HIDDEN))
+            top, mix = mixed(jnp.concatenate(parts, axis=1), rate, cat_v[0:seen, :])
+
+            both_top = jnp.maximum(top, fine_top)
+            if doc:
+                before = p0 + lax.broadcasted_iota(jnp.int32, (step, 1), 0) < b0
+                both_top = jnp.where(before, both_top, top)
+                fine_share = jnp.where(before, jnp.exp2((fine_top - both_top) * rate), 0.0)
+            else:
+                fine_share = jnp.exp2((fine_top - both_top) * rate)
+            share_own = jnp.exp2((top - both_top) * rate)
+            total = mix * share_own + fine_mix * fine_share
+            out_ref[p0 : p0 + step, :] = (total[:, 0:width] / total[:, width:]).astype(bf16)
+
+    @pl.when((b0 >= seg_rows) & (s1 <= 0))
+    def _():
+        attend(False, False)
+
+    @pl.when((b0 < seg_rows) & (s1 <= 0))
+    def _():
+        attend(True, False)
+
+    @pl.when(s1 > 0)
+    def _():
+        attend(True, True)
+
+    cat_k[0:comp_rows, :] = comp_k_ref[0]
+    cat_v[0:comp_rows, 0:width] = comp_v_ref[0]
+
+
+def attend_all(starts, seg_at, recv, conv_keys, conv_values, share):
+    seg_count, seq_count, block, width = recv.shape
+    rows = (block - 2 * share) // 3
+    seg_rows = rows * seq_count
+    comp_rows = seg_rows // RATE
+    step = math.gcd(seg_rows, 256)
+    dims = (rows, share, seg_count, seq_count, step)
+    bf16 = jnp.bfloat16
+    shape = jax.ShapeDtypeStruct
+    per_seg = lambda g, starts, at: (g, 0, 0)
+    conv = pl.BlockSpec((1, RATE * width, width), lambda g, starts, at: (at[0], 0, 0))
+    return pl.pallas_call(
+        functools.partial(attend_kernel, dims),
+        out_shape=(
+            shape((seg_count * seg_rows, width), bf16),
+            shape((seg_count * seg_rows, width), jnp.float32),
+            shape((seg_count, comp_rows, width), bf16),
+            shape((seg_count, comp_rows, width), bf16),
+            shape((seg_count, comp_rows, RATE * width), bf16),
+            shape((seg_count, comp_rows, RATE * width), bf16),
+        ),
+        grid_spec=pltpu.PrefetchScalarGridSpec(
+            num_scalar_prefetch=2,
+            grid=(seg_count,),
+            in_specs=[
+                pl.BlockSpec((1, seq_count, block, width), lambda g, starts, at: (g, 0, 0, 0)),
+                pl.BlockSpec(
+                    (seg_count, seq_count, 2 * share, width),
+                    lambda g, starts, at: (0, 0, 3 * rows // (2 * share), 0),
+                ),
+                conv,
+                conv,
+            ],
+            out_specs=(
+                pl.BlockSpec((seg_rows, width), lambda g, starts, at: (g, 0)),
+                pl.BlockSpec((seg_rows, width), lambda g, starts, at: (g, 0)),
+                pl.BlockSpec((1, comp_rows, width), per_seg),
+                pl.BlockSpec((1, comp_rows, width), per_seg),
+                pl.BlockSpec((1, comp_rows, RATE * width), per_seg),
+                pl.BlockSpec((1, comp_rows, RATE * width), per_seg),
+            ),
+            scratch_shapes=[
+                pltpu.VMEM((seg_rows, width), bf16),
+                pltpu.VMEM((seg_rows, 2 * width), bf16),
+                pltpu.VMEM((comp_rows + seg_rows, width), bf16),
+                pltpu.VMEM((comp_rows + seg_rows, 2 * width), bf16),
+                pltpu.VMEM((seg_rows, width), jnp.float32),
+            ],
+        ),
+        compiler_params=on_vmem(),
+        cost_estimate=pl.CostEstimate(
+            flops=16 * seg_count * seg_rows * seg_rows * width, bytes_accessed=2**23, transcendentals=0
+        ),
+        name="attend",
+    )(starts, seg_at, recv, recv, conv_keys, conv_values)
+
+
+def recon_kernel(
+    dims, recv_ref, recon_ref, comp_k_ref, comp_v_ref, win_k_ref, win_v_ref,
+    grad_ref, loss_ref, sums, losses,
+):
+    rows, seq_count = dims
+    g = pl.program_id(0)
+    width = recv_ref.shape[-1]
+    seg_rows = rows * seq_count
+    scale = 1.0 / math.sqrt(width)
+    rate = math.log2(math.e) * scale
+    bf16 = jnp.bfloat16
+
+    @pl.when(g == 0)
+    def _():
+        sums[...] = jnp.zeros_like(sums)
+        losses[...] = jnp.zeros_like(losses)
+
+    q = recv_ref[0, :, 0:rows, :].reshape(seg_rows, width)
+    comp_k, comp_v = comp_k_ref[0], comp_v_ref[0]
+    scores = matmul_t(q, comp_k)
+    top = jnp.max(scores, axis=1, keepdims=True)
+    comp_exp = jnp.exp2((scores - top) * rate)
+    total = jnp.sum(comp_exp, axis=1, keepdims=True)
+    weights = comp_exp.astype(bf16)
+    recon_comp = matmul(weights, comp_v) / total
+    differ = recon_ref[...] - recon_comp
+    losses[...] += jnp.sum(differ * differ, axis=0, keepdims=True)
+    out_grad = (-2.0 * differ / total).astype(bf16)
+    value_rows = t_matmul(weights, out_grad).astype(bf16)
+    inner = matmul_t(out_grad, comp_v)
+    offset = jnp.sum(out_grad.astype(jnp.float32) * recon_comp, axis=1, keepdims=True)
+    score_grad = (comp_exp * (inner - offset)).astype(bf16)
+    key_rows = (t_matmul(score_grad, q) * scale).astype(bf16)
+    sums[0] += t_matmul(win_k_ref[0], key_rows)
+    sums[1] += t_matmul(win_v_ref[0], value_rows)
+
+    @pl.when(g == pl.num_programs(0) - 1)
+    def _():
+        grad_ref[...] = sums[...].astype(bf16)
+        loss_ref[...] = jnp.broadcast_to(jnp.sum(losses[...], keepdims=True), loss_ref.shape)
+
+
+def recon_all(recv, recon, comp_k, comp_v, win_k, win_v, rows):
+    seg_count, seq_count, block, width = recv.shape
+    seg_rows = rows * seq_count
+    comp_rows = seg_rows // RATE
+    per_seg = lambda g: (g, 0, 0)
+    return pl.pallas_call(
+        functools.partial(recon_kernel, (rows, seq_count)),
+        out_shape=(
+            jax.ShapeDtypeStruct((2, RATE * width, width), jnp.bfloat16),
+            jax.ShapeDtypeStruct((8, width), jnp.float32),
+        ),
+        grid=(seg_count,),
+        in_specs=[
+            pl.BlockSpec((1, seq_count, block, width), lambda g: (g, 0, 0, 0)),
+            pl.BlockSpec((seg_rows, width), lambda g: (g, 0)),
+            pl.BlockSpec((1, comp_rows, width), per_seg),
+            pl.BlockSpec((1, comp_rows, width), per_seg),
+            pl.BlockSpec((1, comp_rows, RATE * width), per_seg),
+            pl.BlockSpec((1, comp_rows, RATE * width), per_seg),
+        ],
+        out_specs=(
+            pl.BlockSpec((2, RATE * width, width), lambda g: (0, 0, 0)),
+            pl.BlockSpec((8, width), lambda g: (0, 0)),
+        ),
+        scratch_shapes=[
+            pltpu.VMEM((2, RATE * width, width), jnp.float32),
+            pltpu.VMEM((1, width), jnp.float32),
+        ],
+        compiler_params=on_vmem(),
+        cost_estimate=pl.CostEstimate(
+            flops=4 * seg_count * seg_rows * seg_rows * width, bytes_accessed=2**22, transcendentals=0
+        ),
+        name="recon",
+    )(recv, recon, comp_k, comp_v, win_k, win_v)
+
+
+def gather_kernel(at_ref, in_ref, k_ref, v_ref):
+    del at_ref
+    k_ref[...] = in_ref[0, 0, 0]
+    v_ref[...] = in_ref[0, 0, 1]
+
+
+def comp_outputs(seg_at, comp_k, comp_v):
+    seg_count, comp_rows, width = comp_k.shape
+    me = seg_at[0]
+    both = jnp.stack((comp_k, comp_v), axis=1)
+    arrived = []
+    for step in range(seg_count):
+        to = lax.rem(me + step, seg_count)
+        part = lax.dynamic_slice_in_dim(both, to, 1, 0)
+        if step:
+            route = [(i, (i + step) % seg_count) for i in range(seg_count)]
+            part = lax.ppermute(part, "seg", route)
+        arrived.append(part)
+    arrived = jnp.stack(arrived)
+    shape = jax.ShapeDtypeStruct((comp_rows, seg_count * width), comp_k.dtype)
+    return pl.pallas_call(
+        gather_kernel,
+        out_shape=(shape, shape),
+        grid_spec=pltpu.PrefetchScalarGridSpec(
+            num_scalar_prefetch=1,
+            grid=(seg_count,),
+            in_specs=[
+                pl.BlockSpec(
+                    (1, 1, 2, comp_rows, width),
+                    lambda h, at: (lax.rem(at[0] - h + seg_count, seg_count), 0, 0, 0, 0),
+                )
+            ],
+            out_specs=[pl.BlockSpec((comp_rows, width), lambda h, at: (0, h))] * 2,
+        ),
+        compiler_params=on_vmem(),
+        name="comp_columns",
+    )(seg_at, arrived)
+
+
+def head_on_device(
+    queries, keys, values, prior_keys, prior_values, conv_keys, conv_values, doc_starts
+):
+    seq_count = lax.axis_size("seq")
+    seg_count = lax.axis_size("seg")
+    rows = queries.shape[0]
+    share = rows // seg_count
+    width = conv_keys.shape[2]
+    seg_at = lax.axis_index("seg").astype(jnp.int32).reshape(1)
+
+    packed = pack(
+        seg_at, queries, keys, values, prior_keys, prior_values, seg_count, seq_count
+    )
+    block = packed.shape[2]
+    recv = lax.all_to_all(
+        packed.reshape(seg_count * seq_count, block, width), BOTH, split_axis=0, concat_axis=0, tiled=True
+    ).reshape(packed.shape)
+    attended, recon, comp_k, comp_v, win_k, win_v = attend_all(
+        doc_starts, seg_at, recv, conv_keys, conv_values, share
+    )
+    attended = lax.all_to_all(
+        attended.reshape(seg_count * seq_count, rows, width), BOTH, split_axis=0, concat_axis=0, tiled=True
+    ).reshape(seg_count, seq_count, rows, width)
+    attended = unpack(attended)
+    grads, loss = recon_all(recv, recon, comp_k, comp_v, win_k, win_v, rows)
+    comp_keys, comp_values = comp_outputs(seg_at, comp_k, comp_v)
+    grads = lax.all_gather(grads, "seg").astype(jnp.float32)
+    for axis, count in (("seq", seq_count), ("seg", seg_count)):
+        bit = 1
+        while bit < count:
+            loss = loss + lax.ppermute(loss, axis, [(i, i ^ bit) for i in range(count)])
+            bit *= 2
+    recon_loss = loss[0, 0] / (seg_count * rows * seq_count)
+    return (attended, comp_keys, comp_values, recon_loss, grads[:, 0], grads[:, 1])
 
 
 def shifted_2(block, axis, distance):
@@ -183,8 +589,16 @@
 
 
 def solution(mesh):
+    def body(*arrays):
+        heads, width = arrays[5].shape[0], arrays[5].shape[2]
+        rows = arrays[0].shape[0]
+        by_head = heads == mesh.shape["seg"] and width % 128 == 0
+        by_head = by_head and all(n & (n - 1) == 0 for n in mesh.shape.values())
+        by_head = by_head and heads % 2 == 0 and rows % (16 * heads) == 0 and 256 % rows == 0
+        return (head_on_device if by_head else on_device)(*arrays)
+
     return jax.shard_map(
-        on_device,
+        body,
         mesh=mesh,
         in_specs=(
             P(("seg", "seq"), None),

time: 434 us -> 180 us (0.41)
  matrix products: 95.1 us -> 0 us
  waiting for transfers between devices: 100 us -> 11.8 us
  other arithmetic: 64.7 us -> 2.97 us
  blocking collectives: 39.8 us -> 91.2 us
  local copies, waits for them, and re-layouts: 46.2 us -> 2.99 us
  Pallas kernels: 0 us -> 42.9 us
  loops' own time: 35 us -> 0 us
  starting transfers between devices: 32.6 us -> 12 us
    all_to_all x6 -> x1, waiting for transfers between devices: 100 us -> 0.01 us  [head_on_device(): lax.all_to_all(attended.reshape(seg_count * seq_count, rows, width), BOTH...]
    dot_general x74 -> x0, matrix products: 95.1 us -> none  [the longest x8 31.3 us: attend_block(): jnp.dot(weights.astype(jnp.bfloat16), value_block, preferred_element_type...]
    all_to_all x0 -> x1, blocking collectives: none -> 91.2 us  [head_on_device(): lax.all_to_all(packed.reshape(seg_count * seq_count, block, width), BOTH,...]
    pallas_call x0 -> x5, Pallas kernels: none -> 42.9 us  [the longest x1 18.6 us: attend_all(): pl.pallas_call(functools.partial(attend_kernel, dims), out_shape=(shape((...]
    psum x1 -> x0, blocking collectives: 39.8 us -> none  [on_device(): total_loss = lax.psum(jnp.sum(losses), ('seg', 'seq'))]
    reduce_sum x26 -> x0, other arithmetic: 37.8 us -> none  [the longest x8 31.6 us: attend_block(): row_total = jnp.sum(weights, axis=1, keepdims=True)]
    another operation x6 -> x0, loops' own time: 35 us -> none  [the longest x1 21.3 us: on_device(): lax.map(attend_block, jnp.arange(head_count * block_count, dtype=jnp.int32))]
    all_to_all x6 -> x1, starting transfers between devices: 26.6 us -> 2.65 us  [head_on_device(): lax.all_to_all(attended.reshape(seg_count * seq_count, rows, width), BOTH...]
  transfers between devices with their start and end apart: 9 -> 10, of which waited for: 5 -> 5; matrix products, arithmetic and copies ran while one was open for 20% -> 3% of each run, Pallas kernels for 0% -> 7%
where the time goes in v1:
time: 180 us
  blocking collectives  91.2 us (51%)
  Pallas kernels  42.9 us (24%)
  between operations  15.9 us (9%)
  starting transfers between devices  12 us (7%)
  waiting for transfers between devices  11.8 us (7%)
  local copies, waits for them, and re-layouts  2.99 us (2%)
  other arithmetic  2.97 us (2%)
    all_to_all x1, blocking collectives, head_on_device(): lax.all_to_all(packed.reshape(seg_count * seq_count, block, width), BOTH,...  91.2 us
    pallas_call x1, Pallas kernels, attend_all(): pl.pallas_call(functools.partial(attend_kernel, dims), out_shape=(shape((...  18.6 us
    ppermute x5, waiting for transfers between devices, head_on_device(): loss = loss + lax.ppermute(loss, axis, [(i, i ^ bit) for i in range(count)])  11.8 us
    pallas_call x1, Pallas kernels, recon_all(): pl.pallas_call(functools.partial(recon_kernel, (rows, seq_count)), out_sh...  9.25 us
    ppermute x5, starting transfers between devices, head_on_device(): loss = loss + lax.ppermute(loss, axis, [(i, i ^ bit) for i in range(count)])  6.89 us
    pallas_call x1, Pallas kernels, pack(): pl.pallas_call(functools.partial(pack_kernel, rows, share), out_shape=jax...  6.76 us
    pallas_call x1, Pallas kernels, unpack(): pl.pallas_call(unpack_kernel, out_shape=jax.ShapeDtypeStruct((rows, seg_c...  5.23 us
  transfers between devices with their start and end apart: 10, of which 5 were waited for; matrix products, arithmetic and copies ran while one was open for 3% of the time, Pallas kernels for 7%

profile of v1, /device:TPU:0, one launch (start us, length us, event | category | flops | bytes accessed | tf_op | source)
XLA Modules:
  0.0 179.8 jit_solution(11061645438182477997)
XLA Ops:
  7.2 6.8 %pack.1 = bf16[4,8,448,128]{3,2,1,0:T(8,128)(2,1)} custom-call(s32[1]{0:T(128)} %bitcast.where_ref.at_ref, bf16[128,4096]{1,0:T(8,128)(2,1)} %q_ref.1, bf16[128,4096]{1,0:T(8,128)(2,1)} %k_ref.1, bf16[128,4096]{1,0:T(8,128)(2,1)} %v_ref.1, bf16[128,4096]{1,0:T(8,128)(2,1)} %pk_ref.1, bf16[128,4096]{1,0:T(8,128)(2,1)} %pv_ref.1), custom_call_target="tpu_custom_call" | custom-call | tf_op jit(solution)/shard_map/pack/pallas_call | solution.py:40
  13.9 91.2 %all_to_all.10 = bf16[32,448,128]{2,1,0:T(8,128)(2,1)} all-to-all(bf16[32,448,128]{2,1,0:T(8,128)(2,1)} %bitcast.23), channel_id=1, replica_groups=mesh['seg'=4,'seq'=8] {'seg','seq'}, dimensions={0} | all-to-all | bytes 7340032 | tf_op jit(solution)/shard_map/all_to_all | solution.py:395
  105.1 18.6 %attend.1 = (bf16[4096,128]{1,0:T(8,128)(2,1)}, f32[4096,128]{1,0:T(8,128)}, bf16[4,256,128]{2,1,0:T(8,128)(2,1)}, bf16[4,256,128]{2,1,0:T(8,128)(2,1)}, bf16[4,...) custom-call(s32[4]{0:T(128)} %starts_ref.1, s32[1]{0:T(128)} %bitcast.where_ref.at_ref, ...), custom_call_target="tpu_custom_call" | custom-call | flops 8589934592 | bytes 8388608 | tf_op jit(solution)/shard_map/attend/pallas_call | solution.py:218
  123.7 2.6 %all-to-all-start.1 = ((bf16[32,128,128]{2,1,0:T(8,128)(2,1)}), bf16[32,128,128]{2,1,0:T(8,128)(2,1)S(1)}, u32[]{:S(2)}, u32[]{:S(2)}) async-start(bf16[32,128,128]{2,1,0:T(8,128)(2,1)} %bitcast.29), calls=%async_computation.1 | async-start | bytes 2097152 | tf_op jit(solution)/shard_map/all_to_all | solution.py:401
  126.3 0.2 all-gather.3.cloned.1.call-start
  126.6 0.0 copy-start.1
  126.6 0.0 copy-start.2
  126.6 9.2 %recon.1 = (bf16[2,512,128]{2,1,0:T(8,128)(2,1)}, f32[8,128]{1,0:T(8,128)}) custom-call(bf16[4,8,448,128]{3,2,1,0:T(8,128)(2,1)} %bitcast.26, f32[4096,128]{1,0:T(8,128)} %get-tuple-element.21.recon_ref, bf16[4,256,128]{2,1,0:T(8,128)(2,1)} %get-tuple-element.17.comp_k_ref, bf16[4,256,128]{2,1,0:T(8,128)(2,1)} %get-tuple-element.18.comp_v_ref, ...), custom_call_target="tpu_custom_call" | custom-call | flops 2147483648 | bytes 4194304 | tf_op jit(solution)/shard_map/recon/pallas_call | solution.py:311
  135.8 0.0 all-gather.3.cloned.1.call-update
  135.9 0.0 copy-done.1
  135.9 0.0 copy-done.2
  135.9 0.1 fusion.2
  136.0 1.4 collective-permute-start.2
  137.4 0.0 collective-permute-start
  137.4 0.8 collective-permute-start.1
  138.2 1.5 collective-permute-start.3
  139.7 2.4 %collective-permute-done.3 = f32[8,128]{1,0:T(8,128)S(1)} collective-permute-done((f32[8,128]{1,0:T(8,128)}, f32[8,128]{1,0:T(8,128)S(1)}, u32[]{:S(2)}, u32[]{:S(2)}) %collective-permute-start.3) | collective-permute-done | bytes 4128 | tf_op jit(solution)/shard_map/ppermute | solution.py:411
  142.0 0.7 add.43
  142.7 1.5 collective-permute-start.4
  144.2 2.2 %collective-permute-done.4 = f32[8,128]{1,0:T(8,128)S(1)} collective-permute-done((f32[8,128]{1,0:T(8,128)S(1)}, f32[8,128]{1,0:T(8,128)S(1)}, u32[]{:S(2)}, u32[]{:S(2)}) %collective-permute-start.4) | collective-permute-done | bytes 4128 | tf_op jit(solution)/shard_map/ppermute | solution.py:411
  146.4 2.4 %collective-permute-start.5 = (f32[8,128]{1,0:T(8,128)S(1)}, f32[8,128]{1,0:T(8,128)S(1)}, u32[]{:S(2)}, u32[]{:S(2)}) collective-permute-start(f32[8,128]{1,0:T(8,128)S(1)} %add.44), channel_id=1, source_target_pairs={{0,4},{1,5},{2,6},{3,7},{4,0},{5,1},{6,2},{7,3},{8,12},{9,13},{10,... | collective-permute-start | bytes 12296 | tf_op jit(solution)/shard_map/ppermute | solution.py:411
  148.8 3.9 %collective-permute-done.5 = f32[8,128]{1,0:T(8,128)S(1)} collective-permute-done((f32[8,128]{1,0:T(8,128)S(1)}, f32[8,128]{1,0:T(8,128)S(1)}, u32[]{:S(2)}, u32[]{:S(2)}) %collective-permute-start.5) | collective-permute-done | bytes 4128 | tf_op jit(solution)/shard_map/ppermute | solution.py:411
  152.7 0.0 collective-permute-start.6
  152.7 1.2 collective-permute-done.6
  153.9 1.5 collective-permute-start.7
  155.4 2.1 %collective-permute-done.7 = f32[8,128]{1,0:T(8,128)S(1)} collective-permute-done((f32[8,128]{1,0:T(8,128)S(1)}, f32[8,128]{1,0:T(8,128)S(1)}, u32[]{:S(2)}, u32[]{:S(2)}) %collective-permute-start.7) | collective-permute-done | bytes 4128 | tf_op jit(solution)/shard_map/ppermute | solution.py:411
  157.5 0.5 slice.9
  158.7 0.0 collective-permute-done.2
  158.7 0.0 collective-permute-done
  158.7 0.0 collective-permute-done.1
  158.7 0.9 pad_maximum_fusion.in_ref
  159.6 3.1 %comp_columns.1 = (bf16[256,512]{1,0:T(8,128)(2,1)}, bf16[256,512]{1,0:T(8,128)(2,1)}) custom-call(s32[1]{0:T(128)} %bitcast.where_ref.at_ref, bf16[4,1,2,256,128]{4,3,2,1,0:T(8,128)(2,1)} %pad_maximum_fusion.in_ref), custom_call_target="tpu_custom_call" | custom-call | tf_op jit(solution)/shard_map/comp_columns/pallas_call | solution.py:362
  162.7 0.0 all-gather.3.cloned.1.call-done
  162.7 1.4 convert
  164.1 1.5 slice_bitcast_fusion
  165.6 0.0 all-to-all-done.1
  165.6 0.0 copy-start
  165.6 1.0 copy-done
  166.6 5.2 %unpack.1 = bf16[128,4096]{1,0:T(8,128)(2,1)} custom-call(bf16[4,8,128,128]{3,2,1,0:T(8,128)(2,1)} %bitcast.27), custom_call_target="tpu_custom_call" | custom-call | tf_op jit(solution)/shard_map/unpack/pallas_call | solution.py:62
  (4 shorter events, 0.0 us)
Async XLA Ops:
  123.7 41.9 %all-to-all-start.1 = ((bf16[32,128,128]{2,1,0:T(8,128)(2,1)}), bf16[32,128,128]{2,1,0:T(8,128)(2,1)S(1)}, u32[]{:S(2)}, u32[]{:S(2)}) async-start(bf16[32,128,128]{2,1,0:T(8,128)(2,1)} %bitcast.29), calls=%async_computation.1 | async-start | bytes 2097152 | tf_op jit(solution)/shard_map/all_to_all | solution.py:401
  126.3 36.4 %all-gather.3.cloned.1.call-start = ((), (), s32[]{:S(2)}) async-start(), calls=%async_computation.2 | async-start | bytes 1310720 | tf_op jit(solution)/shard_map/all_gather | solution.py:407
  126.6 9.3 %copy-start.1 = (bf16[4,256,128]{2,1,0:T(8,128)(2,1)S(1)}, bf16[4,256,128]{2,1,0:T(8,128)(2,1)}, u32[]{:S(2)}) copy-start(bf16[4,256,128]{2,1,0:T(8,128)(2,1)} %get-tuple-element.17.comp_k_ref) | copy-start | bytes 786436
  126.6 9.3 %copy-start.2 = (bf16[4,256,128]{2,1,0:T(8,128)(2,1)S(1)}, bf16[4,256,128]{2,1,0:T(8,128)(2,1)}, u32[]{:S(2)}) copy-start(bf16[4,256,128]{2,1,0:T(8,128)(2,1)} %get-tuple-element.18.comp_v_ref) | copy-start | bytes 786436
  136.0 22.7 %collective-permute-start.2 = (bf16[1,2,256,128]{3,2,1,0:T(8,128)(2,1)S(1)}, bf16[1,2,256,128]{3,2,1,0:T(8,128)(2,1)S(1)}, u32[]{:S(2)}, u32[]{:S(2)}) collective-permute-start(bf16[1,2,256,128]{3,2,1,0:T(8,128)(2,1)S(1)} %get-tuple-element.31), channel_id=1, source_target_pairs={{0,24},{8,0},{16,8},{24,16},{1,25},{9,1},{17,9},{25,17},{2,26},{10... | collective-permute-start | bytes 393224 | tf_op jit(solution)/shard_map/ppermute | solution.py:358
  137.4 21.3 %collective-permute-start = (bf16[1,2,256,128]{3,2,1,0:T(8,128)(2,1)S(1)}, bf16[1,2,256,128]{3,2,1,0:T(8,128)(2,1)S(1)}, u32[]{:S(2)}, u32[]{:S(2)}) collective-permute-start(bf16[1,2,256,128]{3,2,1,0:T(8,128)(2,1)S(1)} %get-tuple-element.29), channel_id=1, source_target_pairs={{0,8},{8,16},{16,24},{24,0},{1,9},{9,17},{17,25},{25,1},{2,10},{10... | collective-permute-start | bytes 393224 | tf_op jit(solution)/shard_map/ppermute | solution.py:358
  137.4 21.3 %collective-permute-start.1 = (bf16[1,2,256,128]{3,2,1,0:T(8,128)(2,1)S(1)}, bf16[1,2,256,128]{3,2,1,0:T(8,128)(2,1)S(1)}, u32[]{:S(2)}, u32[]{:S(2)}) collective-permute-start(bf16[1,2,256,128]{3,2,1,0:T(8,128)(2,1)S(1)} %get-tuple-element.30), channel_id=1, source_target_pairs={{0,16},{8,24},{16,0},{24,8},{1,17},{9,25},{17,1},{25,9},{2,18},{10... | collective-permute-start | bytes 393224 | tf_op jit(solution)/shard_map/ppermute | solution.py:358
  138.2 3.9 %collective-permute-start.3 = (f32[8,128]{1,0:T(8,128)}, f32[8,128]{1,0:T(8,128)S(1)}, u32[]{:S(2)}, u32[]{:S(2)}) collective-permute-start(f32[8,128]{1,0:T(8,128)} %get-tuple-element.24), channel_id=1, source_target_pairs={{0,1},{1,0},{2,3},{3,2},{4,5},{5,4},{6,7},{7,6},{8,9},{9,8},{10,11... | collective-permute-start | bytes 12296 | tf_op jit(solution)/shard_map/ppermute | solution.py:411
  142.7 3.6 %collective-permute-start.4 = (f32[8,128]{1,0:T(8,128)S(1)}, f32[8,128]{1,0:T(8,128)S(1)}, u32[]{:S(2)}, u32[]{:S(2)}) collective-permute-start(f32[8,128]{1,0:T(8,128)S(1)} %add.43), channel_id=1, source_target_pairs={{0,2},{1,3},{2,0},{3,1},{4,6},{5,7},{6,4},{7,5},{8,10},{9,11},{10,... | collective-permute-start | bytes 12296 | tf_op jit(solution)/shard_map/ppermute | solution.py:411
  146.4 6.4 %collective-permute-start.5 = (f32[8,128]{1,0:T(8,128)S(1)}, f32[8,128]{1,0:T(8,128)S(1)}, u32[]{:S(2)}, u32[]{:S(2)}) collective-permute-start(f32[8,128]{1,0:T(8,128)S(1)} %add.44), channel_id=1, source_target_pairs={{0,4},{1,5},{2,6},{3,7},{4,0},{5,1},{6,2},{7,3},{8,12},{9,13},{10,... | collective-permute-start | bytes 12296 | tf_op jit(solution)/shard_map/ppermute | solution.py:411
  152.7 1.2 collective-permute-start.6
  153.9 3.6 %collective-permute-start.7 = (f32[8,128]{1,0:T(8,128)S(1)}, f32[8,128]{1,0:T(8,128)S(1)}, u32[]{:S(2)}, u32[]{:S(2)}) collective-permute-start(f32[8,128]{1,0:T(8,128)S(1)} %add.46), channel_id=1, source_target_pairs={{0,16},{8,24},{16,0},{24,8},{1,17},{9,25},{17,1},{25,9},{2,18},{10... | collective-permute-start | bytes 12296 | tf_op jit(solution)/shard_map/ppermute | solution.py:411
  165.6 1.0 copy-start
Sparse Core Ops, SparseCore 0:
  136.0 20.0 all-gather.2

commit v2 on v0

--- a/solution.py
+++ b/solution.py
@@ -1,11 +1,460 @@
+import functools
 import math
 
 import jax
 import jax.numpy as jnp
 from jax import lax
+from jax.experimental import pallas as pl
+from jax.experimental.pallas import tpu as pltpu
 from jax.sharding import PartitionSpec as P
 
 RATE = 4
+HIDDEN = -1e30
+BOTH = ("seg", "seq")
+
+
+def on_vmem(limit_mib=60):
+    return pltpu.CompilerParams(vmem_limit_bytes=limit_mib * 2**20)
+
+
+def pack_kernel(at_ref, *refs):
+    del at_ref
+    out_ref = refs[-1]
+    seg_count, seq_count, _, width = out_ref.shape
+    for s in range(seq_count):
+        for r in range(seg_count):
+            column = (s * seg_count + r) * width
+            row = 0
+            for ref in refs[:-1]:
+                rows = ref.shape[0]
+                out_ref[r, s, row : row + rows, :] = ref[:, column : column + width]
+                row += rows
+
+
+def pack(at, arrays, prior_arrays, seg_count, seq_count):
+    rows, columns = arrays[0].shape
+    width = columns // (seg_count * seq_count)
+    share = rows // seg_count
+    block = len(arrays) * rows + len(prior_arrays) * share
+    steps = 2
+    wide = columns // steps
+    return pl.pallas_call(
+        pack_kernel,
+        out_shape=jax.ShapeDtypeStruct((seg_count, seq_count, block, width), arrays[0].dtype),
+        grid_spec=pltpu.PrefetchScalarGridSpec(
+            num_scalar_prefetch=1,
+            grid=(steps,),
+            in_specs=[
+                *[pl.BlockSpec((rows, wide), lambda s, at: (0, s))] * len(arrays),
+                *[pl.BlockSpec((share, wide), lambda s, at: (at[0], s))] * len(prior_arrays),
+            ],
+            out_specs=pl.BlockSpec(
+                (seg_count, seq_count // steps, block, width), lambda s, at: (0, s, 0, 0)
+            ),
+        ),
+        compiler_params=on_vmem(),
+        name="pack",
+    )(at, *arrays, *prior_arrays)
+
+
+def unpack_kernel(positions, in_ref, out_ref, loss_ref, rows_ref, tails, sems):
+    seg_count, seq_count, _, width = in_ref.shape
+    rows = rows_ref.shape[0]
+    copies = []
+    for s in range(seq_count):
+        for r in range(seg_count):
+            at = s * seg_count + r
+            columns = slice(at * width, (at + 1) * width)
+            from_ref = in_ref.at[r, s, 0:rows, :]
+            copies.append(pltpu.make_async_copy(from_ref, rows_ref.at[:, columns], sems.at[at]))
+            copies[-1].start()
+    spare = tails.shape[2]
+    tail = pltpu.make_async_copy(
+        in_ref.at[:, :, rows : rows + spare, :], tails, sems.at[seg_count * seq_count]
+    )
+    tail.start()
+    for copy in copies:
+        copy.wait()
+    copy = pltpu.make_async_copy(rows_ref, out_ref, sems.at[seg_count * seq_count + 1])
+    copy.start()
+    tail.wait()
+    parts = tails[...].reshape(-1, width).astype(jnp.float32)
+    total = jnp.sum(jnp.sum(parts, axis=0, keepdims=True), axis=1, keepdims=True)
+    loss_ref[...] = total / positions
+    copy.wait()
+
+
+def unpack(blocks, rows, positions):
+    seg_count, seq_count, _, width = blocks.shape
+    spare = blocks.shape[2] - rows
+    shape = (rows, seg_count * seq_count * width)
+    return pl.pallas_call(
+        functools.partial(unpack_kernel, positions),
+        out_shape=(
+            jax.ShapeDtypeStruct(shape, blocks.dtype),
+            jax.ShapeDtypeStruct((1, 1), jnp.float32),
+        ),
+        in_specs=[pl.BlockSpec(memory_space=pl.ANY)],
+        out_specs=(
+            pl.BlockSpec(memory_space=pl.ANY),
+            pl.BlockSpec(memory_space=pltpu.VMEM),
+        ),
+        scratch_shapes=[
+            pltpu.VMEM(shape, blocks.dtype),
+            pltpu.VMEM((seg_count, seq_count, spare, width), blocks.dtype),
+            pltpu.SemaphoreType.DMA((seg_count * seq_count + 2,)),
+        ],
+        compiler_params=on_vmem(8),
+        name="unpack",
+    )(blocks)
+
+
+def matmul_t(a, b):
+    return lax.dot_general(a, b, (((1,), (1,)), ((), ())), preferred_element_type=jnp.float32)
+
+
+def t_matmul(a, b):
+    return lax.dot_general(a, b, (((0,), (0,)), ((), ())), preferred_element_type=jnp.float32)
+
+
+def matmul(a, b):
+    return jnp.dot(a, b, preferred_element_type=jnp.float32)
+
+
+def softmax_part(scores, rate):
+    top = jnp.max(scores, axis=1, keepdims=True)
+    return top, jnp.exp2((scores - top) * rate)
+
+
+def merge_taps(fine, conv, comp, win, rows_f32):
+    comp_rows, width = comp.shape
+    rows_f32[...] = fine[:, 0:width].astype(jnp.float32)
+    for r in range(RATE):
+        taps = rows_f32[pl.ds(r, comp_rows, stride=RATE), :]
+        win[:, r * width : (r + 1) * width] = taps.astype(jnp.bfloat16)
+    comp[...] = matmul(win[...], conv[0]).astype(jnp.bfloat16)
+
+
+def doc_bounds(starts_ref, g, seg_rows, comp_rows):
+    def start_of(i):
+        return jnp.where(i >= 0, starts_ref[jnp.maximum(i, 0)], seg_rows)
+
+    b0, b1, b2 = start_of(g), start_of(g - 1), start_of(g - 2)
+    s1 = jnp.where(b1 < seg_rows, b1, 0)
+    s2 = jnp.where(b2 < seg_rows, b2, 0)
+    memory_from = jnp.where((g >= 1) & (b1 >= seg_rows), s2, RATE * comp_rows)
+    return b0, s1, memory_from
+
+
+def memory_scores(scores, p0, b0, memory_from):
+    place_q = p0 + lax.broadcasted_iota(jnp.int32, scores.shape, 0)
+    place_k = RATE * lax.broadcasted_iota(jnp.int32, scores.shape, 1)
+    return jnp.where((place_q < b0) & (place_k >= memory_from), scores, HIDDEN)
+
+
+def own_scores(scores, p0, b0):
+    place_q = p0 + lax.broadcasted_iota(jnp.int32, scores.shape, 0)
+    place_k = lax.broadcasted_iota(jnp.int32, scores.shape, 1)
+    seen = (place_k <= place_q) & ((place_k >= b0) | (place_q < b0))
+    return jnp.where(seen, scores, HIDDEN)
+
+
+def before_doc(step, p0, b0):
+    return p0 + lax.broadcasted_iota(jnp.int32, (step, 1), 0) < b0
+
+
+def head_kernel(
+    dims, starts_ref, at_ref, recv_ref, prior_ref, conv_k_ref, conv_v_ref,
+    out_ref, *rest,
+):
+    rows, seq_count, step = dims
+    share_refs, rest = rest[: prior_ref.shape[0]], rest[prior_ref.shape[0] :]
+    (
+        out_rows, loss_rows, comp_ref, fine_k, fine_v, cat_k, cat_v, rows_f32,
+        win_k, win_v, comp_w, out_grads, score_grads, sums, losses, sems,
+    ) = rest
+    g = pl.program_id(0)
+    seg_rows = rows * seq_count
+    comp_rows = seg_rows // RATE
+    seg_count, _, both_shares, width = prior_ref.shape
+    share = both_shares // 2
+    scale = 1.0 / math.sqrt(width)
+    rate = math.log2(math.e) * scale
+    bf16 = jnp.bfloat16
+
+    @pl.when(g == 0)
+    def _():
+        cat_k[0:comp_rows, :] = jnp.zeros((comp_rows, width), bf16)
+        cat_v[0:comp_rows, 0:width] = jnp.zeros((comp_rows, width), bf16)
+        cat_v[:, width:] = jnp.ones((comp_rows + seg_rows, width), bf16)
+        fine_v[:, width:] = jnp.ones((seg_rows, width), bf16)
+        sums[...] = jnp.zeros_like(sums)
+        losses[...] = jnp.zeros_like(losses)
+        for s in range(seq_count):
+            for i in range(seg_count):
+                at = s * rows + i * share
+                fine_k[at : at + share, :] = prior_ref[i, s, 0:share, :]
+                fine_v[at : at + share, 0:width] = prior_ref[i, s, share:, :]
+
+    @pl.when(g > 0)
+    def _():
+        fine_k[...] = cat_k[comp_rows:, :]
+        fine_v[:, 0:width] = cat_v[comp_rows:, 0:width]
+
+    cat_k[comp_rows:, :] = recv_ref[0, :, rows : 2 * rows, :].reshape(seg_rows, width)
+    cat_v[comp_rows:, 0:width] = recv_ref[0, :, 2 * rows : 3 * rows, :].reshape(seg_rows, width)
+    merge_taps(fine_k, conv_k_ref, comp_ref.at[0], win_k, rows_f32)
+    merge_taps(fine_v, conv_v_ref, comp_ref.at[1], win_v, rows_f32)
+    comp_k, comp_v = comp_ref[0], comp_ref[1]
+    for i, share_ref in enumerate(share_refs):
+
+        @pl.when(lax.rem(g - at_ref[0] + seg_count, seg_count) == i)
+        def _():
+            share_ref[0 : 2 * comp_rows, :] = comp_ref[...].reshape(2 * comp_rows, width)
+
+    b0, s1, memory_from = doc_bounds(starts_ref, g, seg_rows, comp_rows)
+
+    def queries(p0):
+        return recv_ref[0, p0 // rows : (p0 + step) // rows, 0:rows, :].reshape(step, width)
+
+    def weighted(weights, values_and_ones):
+        mix = matmul(weights.astype(bf16), values_and_ones)
+        return mix[:, 0:width], mix[:, width:]
+
+    def attend(fine_from_s1):
+        fine, recon = {}, {}
+
+        def fine_scores(p0):
+            return matmul_t(queries(p0), fine_k[...])
+
+        def fine_part(p0, scores):
+            top, weights = softmax_part(scores, rate)
+            mix, total = weighted(weights, fine_v[...])
+            recon[p0] = mix / total
+            if fine_from_s1:
+                place = lax.broadcasted_iota(jnp.int32, scores.shape, 1)
+                top, weights = softmax_part(jnp.where(place >= s1, scores, HIDDEN), rate)
+                mix, total = weighted(weights, fine_v[...])
+            fine[p0] = top, mix, total
+
+        def comp_scores(p0):
+            return matmul_t(queries(p0), comp_k)
+
+        def comp_part(p0, scores):
+            here = slice(p0, p0 + step)
+            _, comp_exp = softmax_part(scores, rate)
+            total = jnp.sum(comp_exp, axis=1, keepdims=True)
+            weights = comp_exp.astype(bf16)
+            recon_comp = matmul(weights, comp_v) / total
+            differ = recon.pop(p0) - recon_comp
+            losses[...] += jnp.sum(differ * differ, axis=0, keepdims=True)
+            out_grad = (-2.0 * differ / total).astype(bf16)
+            inner = matmul_t(out_grad, comp_v)
+            offset = jnp.sum(out_grad.astype(jnp.float32) * recon_comp, axis=1, keepdims=True)
+            comp_w[here, :] = weights
+            out_grads[here, :] = out_grad
+            score_grads[here, :] = (comp_exp * (inner - offset)).astype(bf16)
+
+        def cat_scores(p0):
+            scores = matmul_t(queries(p0), cat_k[0 : comp_rows + p0 + step, :])
+            memory = memory_scores(scores[:, 0:comp_rows], p0, b0, memory_from)
+            return jnp.concatenate((memory, own_scores(scores[:, comp_rows:], p0, b0)), axis=1)
+
+        def cat_part(p0, scores):
+            top, weights = softmax_part(scores, rate)
+            mix, total = weighted(weights, cat_v[0 : comp_rows + p0 + step, :])
+            fine_top, fine_mix, fine_total = fine.pop(p0)
+            seen = before_doc(step, p0, b0)
+            both = jnp.where(seen, jnp.maximum(top, fine_top), top)
+            fine_share = jnp.where(seen, jnp.exp2((fine_top - both) * rate), 0.0)
+            cat_share = jnp.exp2((top - both) * rate)
+            mix = mix * cat_share + fine_mix * fine_share
+            total = total * cat_share + fine_total * fine_share
+            here = slice(p0 // rows, (p0 + step) // rows)
+            out_rows[g, here] = (mix / total).astype(bf16).reshape(step // rows, rows, width)
+
+        parts = [
+            (p0, *part)
+            for p0 in range(0, seg_rows, step)
+            for part in ((fine_scores, fine_part), (cat_scores, cat_part), (comp_scores, comp_part))
+        ]
+        ahead = parts[0][1](parts[0][0])
+        for i, (p0, _, finish) in enumerate(parts):
+            scores = ahead
+            if i + 1 < len(parts):
+                ahead = parts[i + 1][1](parts[i + 1][0])
+            finish(p0, scores)
+
+    @pl.when(s1 <= 0)
+    def _():
+        attend(False)
+
+    @pl.when(s1 > 0)
+    def _():
+        attend(True)
+
+    def copy_out(i):
+        return pltpu.make_async_copy(out_rows.at[i], out_ref.at[i, :, 0:rows, :], sems.at[i])
+
+    copy_out(g).start()
+    cat_k[0:comp_rows, :] = comp_k
+    cat_v[0:comp_rows, 0:width] = comp_v
+    q = recv_ref[0, :, 0:rows, :].reshape(seg_rows, width)
+    value_rows = t_matmul(comp_w[...], out_grads[...]).astype(bf16)
+    key_rows = (t_matmul(score_grads[...], q) * scale).astype(bf16)
+    sums[0] += t_matmul(win_k[...], key_rows)
+    sums[1] += t_matmul(win_v[...], value_rows)
+
+    @pl.when(g == seg_count - 1)
+    def _():
+        left = losses[...]
+        parts = []
+        for _ in range(3):
+            parts.append(left.astype(bf16).astype(jnp.float32))
+            left = left - parts[-1]
+        spare = loss_rows.shape[2]
+        parts.append(jnp.zeros((spare - len(parts), width), jnp.float32))
+        tail = jnp.concatenate(parts).astype(bf16)
+        for s in range(seq_count):
+            loss_rows[0, s] = tail
+        copies = [
+            pltpu.make_async_copy(
+                loss_rows.at[0], out_ref.at[i, :, rows : rows + spare, :], sems.at[seg_count + i]
+            )
+            for i in range(seg_count)
+        ]
+        for copy in copies:
+            copy.start()
+        grads = sums[...].astype(bf16).reshape(-1, width)
+        for share_ref in share_refs:
+            share_ref[2 * comp_rows :, :] = grads
+        for i in range(seg_count):
+            copy_out(i).wait()
+        for copy in copies:
+            copy.wait()
+
+
+def head(starts, at, recv, conv_keys, conv_values):
+    seg_count, seq_count, block, width = recv.shape
+    rows = block * seg_count // (3 * seg_count + 2)
+    share = rows // seg_count
+    seg_rows = rows * seq_count
+    comp_rows = seg_rows // RATE
+    step = math.gcd(seg_rows, 256)
+    bf16, f32 = jnp.bfloat16, jnp.float32
+    shape = jax.ShapeDtypeStruct
+    spare = 16
+    share_shape = (2 * comp_rows + 2 * RATE * width, width)
+    conv = pl.BlockSpec((1, RATE * width, width), lambda g, starts, at: (at[0], 0, 0))
+
+    def body(starts_ref, at_ref, *refs):
+        head_kernel((rows, seq_count, step), starts_ref, at_ref, *refs)
+
+    return pl.pallas_call(
+        body,
+        out_shape=(
+            shape((seg_count, seq_count, rows + spare, width), bf16),
+            *[shape(share_shape, bf16)] * seg_count,
+        ),
+        grid_spec=pltpu.PrefetchScalarGridSpec(
+            num_scalar_prefetch=2,
+            grid=(seg_count,),
+            in_specs=[
+                pl.BlockSpec((1, seq_count, 3 * rows, width), lambda g, starts, at: (g, 0, 0, 0)),
+                pl.BlockSpec(
+                    (seg_count, seq_count, 2 * share, width),
+                    lambda g, starts, at: (0, 0, 3 * rows // (2 * share), 0),
+                ),
+                conv,
+                conv,
+            ],
+            out_specs=(
+                pl.BlockSpec(memory_space=pl.ANY),
+                *[pl.BlockSpec(share_shape, lambda g, starts, at: (0, 0))] * seg_count,
+            ),
+            scratch_shapes=[
+                pltpu.VMEM((seg_count, seq_count, rows, width), bf16),
+                pltpu.VMEM((1, seq_count, spare, width), bf16),
+                pltpu.VMEM((2, comp_rows, width), bf16),
+                pltpu.VMEM((seg_rows, width), bf16),
+                pltpu.VMEM((seg_rows, 2 * width), bf16),
+                pltpu.VMEM((comp_rows + seg_rows, width), bf16),
+                pltpu.VMEM((comp_rows + seg_rows, 2 * width), bf16),
+                pltpu.VMEM((seg_rows, width), f32),
+                pltpu.VMEM((comp_rows, RATE * width), bf16),
+                pltpu.VMEM((comp_rows, RATE * width), bf16),
+                pltpu.VMEM((seg_rows, comp_rows), bf16),
+                pltpu.VMEM((seg_rows, width), bf16),
+                pltpu.VMEM((seg_rows, comp_rows), bf16),
+                pltpu.VMEM((2, RATE * width, width), f32),
+                pltpu.VMEM((1, width), f32),
+                pltpu.SemaphoreType.DMA((2 * seg_count,)),
+            ],
+        ),
+        compiler_params=on_vmem(28),
+        cost_estimate=pl.CostEstimate(
+            flops=20 * seg_count * seg_rows * seg_rows * width, bytes_accessed=2**23, transcendentals=0
+        ),
+        name="head",
+    )(starts, at, recv, recv, conv_keys, conv_values)
+
+
+def share_kernel(at_ref, *refs):
+    shares, (comp_k_ref, comp_v_ref, grad_k_ref, grad_v_ref) = refs[:-4], refs[-4:]
+    heads, taps, width = grad_k_ref.shape
+    comp_rows = comp_k_ref.shape[0]
+    for step, ref in enumerate(shares):
+        head_at = lax.rem(at_ref[0] - step + heads, heads)
+        columns = pl.ds(pl.multiple_of(head_at * width, width), width)
+        comp_k_ref[:, columns] = ref[0:comp_rows, :]
+        comp_v_ref[:, columns] = ref[comp_rows : 2 * comp_rows, :]
+        grads = ref[2 * comp_rows :, :].astype(jnp.float32)
+        grad_k_ref[head_at] = grads[0:taps]
+        grad_v_ref[head_at] = grads[taps:]
+
+
+def shared(at, shares, comp_rows, taps):
+    heads = len(shares)
+    width = shares[0].shape[1]
+    arrived = [shares[0]]
+    for step in range(1, heads):
+        route = [(i, (i + step) % heads) for i in range(heads)]
+        arrived.append(lax.ppermute(shares[step], "seg", route))
+    comp = jax.ShapeDtypeStruct((comp_rows, heads * width), shares[0].dtype)
+    grad = jax.ShapeDtypeStruct((heads, taps, width), jnp.float32)
+    in_vmem = pl.BlockSpec(memory_space=pltpu.VMEM)
+    return pl.pallas_call(
+        share_kernel,
+        out_shape=(comp, comp, grad, grad),
+        in_specs=[pl.BlockSpec(memory_space=pltpu.SMEM), *[in_vmem] * heads],
+        out_specs=(in_vmem,) * 4,
+        compiler_params=on_vmem(12),
+        name="shared",
+    )(at, *arrived)
+
+
+def head_on_device(
+    queries, keys, values, prior_keys, prior_values, conv_keys, conv_values, doc_starts
+):
+    seq_count = lax.axis_size("seq")
+    seg_count = lax.axis_size("seg")
+    count = seg_count * seq_count
+    rows = queries.shape[0]
+    width = conv_keys.shape[2]
+    at = lax.axis_index("seg").astype(jnp.int32).reshape(1)
+
+    def exchanged(blocks):
+        flat = blocks.reshape(count, -1, width)
+        flat = lax.all_to_all(flat, BOTH, split_axis=0, concat_axis=0, tiled=True)
+        return flat.reshape(blocks.shape)
+
+    packed = pack(at, (queries, keys, values), (prior_keys, prior_values), seg_count, seq_count)
+    attended, *shares = head(doc_starts, at, exchanged(packed), conv_keys, conv_values)
+    attended, loss = unpack(exchanged(attended), rows, count * rows)
+    comp_keys, comp_values, grad_k, grad_v = shared(
+        at, shares, rows * seq_count // RATE, conv_keys.shape[1]
+    )
+    return (attended, comp_keys, comp_values, loss[0, 0], grad_k, grad_v)
 
 
 def shifted_2(block, axis, distance):
@@ -183,8 +632,16 @@
 
 
 def solution(mesh):
+    def body(*arrays):
+        heads, width = arrays[5].shape[0], arrays[5].shape[2]
+        rows = arrays[0].shape[0]
+        by_head = heads == mesh.shape["seg"] and width % 128 == 0
+        by_head = by_head and all(n & (n - 1) == 0 for n in mesh.shape.values())
+        by_head = by_head and heads % 2 == 0 and rows % (16 * heads) == 0 and 256 % rows == 0
+        return (head_on_device if by_head else on_device)(*arrays)
+
     return jax.shard_map(
-        on_device,
+        body,
         mesh=mesh,
         in_specs=(
             P(("seg", "seq"), None),

time: 434 us -> 155 us (0.36)
  matrix products: 95.1 us -> 0 us
  waiting for transfers between devices: 100 us -> 26.9 us
  other arithmetic: 64.7 us -> 0 us
  blocking collectives: 39.8 us -> 91.1 us
  local copies, waits for them, and re-layouts: 46.2 us -> 0.01 us
  loops' own time: 35 us -> 0 us
  Pallas kernels: 0 us -> 28.8 us
  starting transfers between devices: 32.6 us -> 5.83 us
  between operations: 17.4 us -> 0.67 us
    all_to_all x6 -> x1, waiting for transfers between devices: 100 us -> 0.01 us  [exchanged(): flat = lax.all_to_all(flat, BOTH, split_axis=0, concat_axis=0, tiled=True)]
    dot_general x74 -> x0, matrix products: 95.1 us -> none  [the longest x8 31.3 us: attend_block(): jnp.dot(weights.astype(jnp.bfloat16), value_block, preferred_element_type...]
    all_to_all x0 -> x1, blocking collectives: none -> 91.1 us  [exchanged(): flat = lax.all_to_all(flat, BOTH, split_axis=0, concat_axis=0, tiled=True)]
    psum x1 -> x0, blocking collectives: 39.8 us -> none  [on_device(): total_loss = lax.psum(jnp.sum(losses), ('seg', 'seq'))]
    reduce_sum x26 -> x0, other arithmetic: 37.8 us -> none  [the longest x8 31.6 us: attend_block(): row_total = jnp.sum(weights, axis=1, keepdims=True)]
    another operation x6 -> x0, loops' own time: 35 us -> none  [the longest x1 21.3 us: on_device(): lax.map(attend_block, jnp.arange(head_count * block_count, dtype=jnp.int32))]
    pallas_call x0 -> x4, Pallas kernels: none -> 28.8 us  [the longest x1 21.4 us: head(): pl.pallas_call(body, out_shape=(shape((seg_count, seq_count, rows + spare...]
    ppermute x2 -> x3, waiting for transfers between devices: 0.01 us -> 26.9 us  [shared(): arrived.append(lax.ppermute(shares[step], 'seg', route))]
  transfers between devices with their start and end apart: 9 -> 4, of which waited for: 5 -> 3; matrix products, arithmetic and copies ran while one was open for 20% -> 0% of each run, Pallas kernels for 0% -> 1%
where the time goes in v2:
time: 155 us; the launch traced here: 153 us
  blocking collectives  91.1 us (59%)
  Pallas kernels  28.8 us (19%)
  waiting for transfers between devices  26.9 us (17%)
  starting transfers between devices  5.83 us (4%)
    all_to_all x1, blocking collectives, exchanged(): flat = lax.all_to_all(flat, BOTH, split_axis=0, concat_axis=0, tiled=True)  91.1 us
    ppermute x3, waiting for transfers between devices, shared(): arrived.append(lax.ppermute(shares[step], 'seg', route))  26.9 us
    pallas_call x1, Pallas kernels, head(): pl.pallas_call(body, out_shape=(shape((seg_count, seq_count, rows + spare...  21.4 us
    pallas_call x1, Pallas kernels, pack(): pl.pallas_call(pack_kernel, out_shape=jax.ShapeDtypeStruct((seg_count, se...  3.55 us
    ppermute x3, starting transfers between devices, shared(): arrived.append(lax.ppermute(shares[step], 'seg', route))  3.15 us
  transfers between devices with their start and end apart: 4, of which 3 were waited for; matrix products, arithmetic and copies ran while one was open for 0% of the time, Pallas kernels for 1%

profile of v2, /device:TPU:0, one launch (start us, length us, event | category | flops | bytes accessed | tf_op | source)
XLA Modules:
  0.0 153.3 jit_solution(17016085111091809826)
XLA Ops:
  0.6 3.6 %pack.1 = bf16[4,8,448,128]{3,2,1,0:T(8,128)(2,1)} custom-call(s32[1]{0:T(128)} %bitcast.at_ref, bf16[128,4096]{1,0:T(8,128)(2,1)} %refs_0_.1, bf16[128,4096]{1,0:T(8,128)(2,1)} %refs_1_.1, bf16[128,4096]{1,0:T(8,128)(2,1)} %refs_2_.2, bf16[128,4096]{1,0:T(8,128)(2,1)} %refs_3_.2, bf16[128,4096]{1,0:T(8,128)(2,1)} %refs_4_.1), custom_call_target="tpu_custom_call" | custom-call | tf_op jit(solution)/shard_map/pack/pallas_call | solution.py:41
  4.2 0.0 copy-start
  4.2 0.0 copy-start.1
  4.2 0.0 copy-start.2
  4.2 91.1 %all_to_all.10 = bf16[32,448,128]{2,1,0:T(8,128)(2,1)S(1)} all-to-all(bf16[32,448,128]{2,1,0:T(8,128)(2,1)} %bitcast.9), channel_id=1, replica_groups=mesh['seg'=4,'seq'=8] {'seg','seq'}, dimensions={0} | all-to-all | bytes 7340032 | tf_op jit(solution)/shard_map/all_to_all | solution.py:448
  95.3 0.0 copy-done
  95.3 0.0 copy-done.1
  95.3 0.0 copy-done.2
  95.3 21.4 %head.1 = (bf16[4,8,144,128]{3,2,1,0:T(8,128)(2,1)}, bf16[1536,128]{1,0:T(8,128)(2,1)S(1)}, bf16[1536,128]{1,0:T(8,128)(2,1)S(1)}, bf16[1536,128]{1,0:T(8,128)(2,1)S(1)}, bf16[1536,128]{1,0:T(8,128)(2,1)S(1)}) custom-call(s32[4]{0:T(128)S(1)} %copy-done.2, s32[1]{0:T(128)} %bitcast.at_ref, bf16[4,8,448,128]{3,2,1,0:T(8,128)(2,1)S(1)} %bitcast.7, ...), custom_call_target="tpu_custom_call" | custom-call | flops 10737418240 | bytes 8388608 | tf_op jit(solution)/shard_map/head/pallas_call | solution.py:353
  116.7 2.7 %all-to-all-start.1 = ((bf16[32,144,128]{2,1,0:T(8,128)(2,1)}), bf16[32,144,128]{2,1,0:T(8,128)(2,1)S(1)}, u32[]{:S(2)}, u32[]{:S(2)}) async-start(bf16[32,144,128]{2,1,0:T(8,128)(2,1)} %bitcast.3), calls=%async_computation.1 | async-start | bytes 2359296 | tf_op jit(solution)/shard_map/all_to_all | solution.py:448
  119.4 0.2 collective-permute-start
  119.6 1.7 %collective-permute-start.1 = (bf16[1536,128]{1,0:T(8,128)(2,1)S(1)}, bf16[1536,128]{1,0:T(8,128)(2,1)S(1)}, u32[]{:S(2)}, u32[]{:S(2)}) collective-permute-start(bf16[1536,128]{1,0:T(8,128)(2,1)S(1)} %get-tuple-element.21), channel_id=1, source_target_pairs={{0,16},{8,24},{16,0},{24,8},{1,17},{9,25},{17,1},{25,9},{2,18},{10... | collective-permute-start | bytes 1179656 | tf_op jit(solution)/shard_map/ppermute | solution.py:422
  121.2 1.3 collective-permute-start.2
  122.6 17.6 %collective-permute-done.refs_1_ = bf16[1536,128]{1,0:T(8,128)(2,1)S(1)} collective-permute-done((bf16[1536,128]{1,0:T(8,128)(2,1)S(1)}, bf16[1536,128]{1,0:T(8,128)(2,1)S(1)}, u32[]{:S(2)}, u32[]{:S(2)}) %collective-permute-start) | collective-permute-done | bytes 393248 | tf_op jit(solution)/shard_map/ppermute | solution.py:422
  140.1 1.4 collective-permute-done.1.refs_2_
  141.6 7.9 %collective-permute-done.2.refs_3_ = bf16[1536,128]{1,0:T(8,128)(2,1)S(1)} collective-permute-done((bf16[1536,128]{1,0:T(8,128)(2,1)S(1)}, bf16[1536,128]{1,0:T(8,128)(2,1)S(1)}, u32[]{:S(2)}, u32[]{:S(2)}) %collective-permute-start.2) | collective-permute-done | bytes 393248 | tf_op jit(solution)/shard_map/ppermute | solution.py:422
  149.5 1.7 %shared.1 = (bf16[256,512]{1,0:T(8,128)(2,1)}, bf16[256,512]{1,0:T(8,128)(2,1)}, f32[4,512,128]{2,1,0:T(8,128)}, f32[4,512,128]{2,1,0:T(8,128)}) custom-call(s32[1]{0:T(128)} %bitcast.at_ref, bf16[1536,128]{1,0:T(8,128)(2,1)S(1)} %get-tuple-element.19.refs_0_, bf16[1536,128]{1,0:T(8,128)(2,1)S(1)} %collective-permute-done.refs_1_, ...), custom_call_target="tpu_custom_call" | custom-call | tf_op jit(solution)/shard_map/shared/pallas_call | solution.py:426
  151.2 0.0 all-to-all-done.1
  151.2 2.1 %unpack.1 = (bf16[128,4096]{1,0:T(8,128)(2,1)}, f32[1,1]{1,0:T(1,128)}) custom-call(bf16[4,8,144,128]{3,2,1,0:T(8,128)(2,1)S(1)} %bitcast.6), custom_call_target="tpu_custom_call" | custom-call | tf_op jit(solution)/shard_map/unpack/pallas_call | solution.py:91
Async XLA Ops:
  4.2 91.1 %copy-start = (bf16[4,512,128]{2,1,0:T(8,128)(2,1)S(1)}, bf16[4,512,128]{2,1,0:T(8,128)(2,1)}, u32[]{:S(2)}) copy-start(bf16[4,512,128]{2,1,0:T(8,128)(2,1)} %refs_2_.3) | copy-start | bytes 1572868
  4.2 91.1 %copy-start.1 = (bf16[4,512,128]{2,1,0:T(8,128)(2,1)S(1)}, bf16[4,512,128]{2,1,0:T(8,128)(2,1)}, u32[]{:S(2)}) copy-start(bf16[4,512,128]{2,1,0:T(8,128)(2,1)} %refs_3_.3) | copy-start | bytes 1572868
  4.2 91.1 %copy-start.2 = (s32[4]{0:T(128)S(1)}, s32[4]{0:T(128)}, u32[]{:S(2)}) copy-start(s32[4]{0:T(128)} %starts_ref.1) | copy-start | bytes 52
  116.7 34.5 %all-to-all-start.1 = ((bf16[32,144,128]{2,1,0:T(8,128)(2,1)}), bf16[32,144,128]{2,1,0:T(8,128)(2,1)S(1)}, u32[]{:S(2)}, u32[]{:S(2)}) async-start(bf16[32,144,128]{2,1,0:T(8,128)(2,1)} %bitcast.3), calls=%async_computation.1 | async-start | bytes 2359296 | tf_op jit(solution)/shard_map/all_to_all | solution.py:448
  119.4 20.7 %collective-permute-start = (bf16[1536,128]{1,0:T(8,128)(2,1)S(1)}, bf16[1536,128]{1,0:T(8,128)(2,1)S(1)}, u32[]{:S(2)}, u32[]{:S(2)}) collective-permute-start(bf16[1536,128]{1,0:T(8,128)(2,1)S(1)} %get-tuple-element.20), channel_id=1, source_target_pairs={{0,8},{8,16},{16,24},{24,0},{1,9},{9,17},{17,25},{25,1},{2,10},{10... | collective-permute-start | bytes 1179656 | tf_op jit(solution)/shard_map/ppermute | solution.py:422
  119.6 22.0 %collective-permute-start.1 = (bf16[1536,128]{1,0:T(8,128)(2,1)S(1)}, bf16[1536,128]{1,0:T(8,128)(2,1)S(1)}, u32[]{:S(2)}, u32[]{:S(2)}) collective-permute-start(bf16[1536,128]{1,0:T(8,128)(2,1)S(1)} %get-tuple-element.21), channel_id=1, source_target_pairs={{0,16},{8,24},{16,0},{24,8},{1,17},{9,25},{17,1},{25,9},{2,18},{10... | collective-permute-start | bytes 1179656 | tf_op jit(solution)/shard_map/ppermute | solution.py:422
  121.2 28.3 %collective-permute-start.2 = (bf16[1536,128]{1,0:T(8,128)(2,1)S(1)}, bf16[1536,128]{1,0:T(8,128)(2,1)S(1)}, u32[]{:S(2)}, u32[]{:S(2)}) collective-permute-start(bf16[1536,128]{1,0:T(8,128)(2,1)S(1)} %get-tuple-element.22), channel_id=1, source_target_pairs={{0,24},{8,0},{16,8},{24,16},{1,25},{9,1},{17,9},{25,17},{2,26},{10... | collective-permute-start | bytes 1179656 | tf_op jit(solution)/shard_map/ppermute | solution.py:422

commit v3 on v2

--- a/solution.py
+++ b/solution.py
@@ -10,7 +10,9 @@
 
 RATE = 4
 HIDDEN = -1e30
-BOTH = ("seg", "seq")
+STEP = 512
+AHEAD = 2
+BOTH = ("seq", "seg")
 
 
 def on_vmem(limit_mib=60):
@@ -20,14 +22,14 @@
 def pack_kernel(at_ref, *refs):
     del at_ref
     out_ref = refs[-1]
-    seg_count, seq_count, _, width = out_ref.shape
+    seq_count, seg_count, _, width = out_ref.shape
     for s in range(seq_count):
         for r in range(seg_count):
             column = (s * seg_count + r) * width
             row = 0
             for ref in refs[:-1]:
                 rows = ref.shape[0]
-                out_ref[r, s, row : row + rows, :] = ref[:, column : column + width]
+                out_ref[s, r, row : row + rows, :] = ref[:, column : column + width]
                 row += rows
 
 
@@ -40,7 +42,7 @@
     wide = columns // steps
     return pl.pallas_call(
         pack_kernel,
-        out_shape=jax.ShapeDtypeStruct((seg_count, seq_count, block, width), arrays[0].dtype),
+        out_shape=jax.ShapeDtypeStruct((seq_count, seg_count, block, width), arrays[0].dtype),
         grid_spec=pltpu.PrefetchScalarGridSpec(
             num_scalar_prefetch=1,
             grid=(steps,),
@@ -49,7 +51,7 @@
                 *[pl.BlockSpec((share, wide), lambda s, at: (at[0], s))] * len(prior_arrays),
             ],
             out_specs=pl.BlockSpec(
-                (seg_count, seq_count // steps, block, width), lambda s, at: (0, s, 0, 0)
+                (seq_count // steps, seg_count, block, width), lambda s, at: (s, 0, 0, 0)
             ),
         ),
         compiler_params=on_vmem(),
@@ -58,14 +60,14 @@
 
 
 def unpack_kernel(positions, in_ref, out_ref, loss_ref, rows_ref, tails, sems):
-    seg_count, seq_count, _, width = in_ref.shape
+    seq_count, seg_count, _, width = in_ref.shape
     rows = rows_ref.shape[0]
     copies = []
     for s in range(seq_count):
         for r in range(seg_count):
             at = s * seg_count + r
             columns = slice(at * width, (at + 1) * width)
-            from_ref = in_ref.at[r, s, 0:rows, :]
+            from_ref = in_ref.at[s, r, 0:rows, :]
             copies.append(pltpu.make_async_copy(from_ref, rows_ref.at[:, columns], sems.at[at]))
             copies[-1].start()
     spare = tails.shape[2]
@@ -85,7 +87,7 @@
 
 
 def unpack(blocks, rows, positions):
-    seg_count, seq_count, _, width = blocks.shape
+    seq_count, seg_count, _, width = blocks.shape
     spare = blocks.shape[2] - rows
     shape = (rows, seg_count * seq_count * width)
     return pl.pallas_call(
@@ -101,7 +103,7 @@
         ),
         scratch_shapes=[
             pltpu.VMEM(shape, blocks.dtype),
-            pltpu.VMEM((seg_count, seq_count, spare, width), blocks.dtype),
+            pltpu.VMEM((seq_count, seg_count, spare, width), blocks.dtype),
             pltpu.SemaphoreType.DMA((seg_count * seq_count + 2,)),
         ],
         compiler_params=on_vmem(8),
@@ -165,18 +167,18 @@
 
 def head_kernel(
     dims, starts_ref, at_ref, recv_ref, prior_ref, conv_k_ref, conv_v_ref,
-    out_ref, *rest,
+    out_ref, grad_ref, *rest,
 ):
     rows, seq_count, step = dims
-    share_refs, rest = rest[: prior_ref.shape[0]], rest[prior_ref.shape[0] :]
+    share_refs, rest = rest[: prior_ref.shape[1]], rest[prior_ref.shape[1] :]
     (
         out_rows, loss_rows, comp_ref, fine_k, fine_v, cat_k, cat_v, rows_f32,
-        win_k, win_v, comp_w, out_grads, score_grads, sums, losses, sems,
+        win_k, win_v, sums, losses, sems,
     ) = rest
     g = pl.program_id(0)
     seg_rows = rows * seq_count
     comp_rows = seg_rows // RATE
-    seg_count, _, both_shares, width = prior_ref.shape
+    _, seg_count, both_shares, width = prior_ref.shape
     share = both_shares // 2
     scale = 1.0 / math.sqrt(width)
     rate = math.log2(math.e) * scale
@@ -193,16 +195,16 @@
         for s in range(seq_count):
             for i in range(seg_count):
                 at = s * rows + i * share
-                fine_k[at : at + share, :] = prior_ref[i, s, 0:share, :]
-                fine_v[at : at + share, 0:width] = prior_ref[i, s, share:, :]
+                fine_k[at : at + share, :] = prior_ref[s, i, 0:share, :]
+                fine_v[at : at + share, 0:width] = prior_ref[s, i, share:, :]
 
     @pl.when(g > 0)
     def _():
         fine_k[...] = cat_k[comp_rows:, :]
         fine_v[:, 0:width] = cat_v[comp_rows:, 0:width]
 
-    cat_k[comp_rows:, :] = recv_ref[0, :, rows : 2 * rows, :].reshape(seg_rows, width)
-    cat_v[comp_rows:, 0:width] = recv_ref[0, :, 2 * rows : 3 * rows, :].reshape(seg_rows, width)
+    cat_k[comp_rows:, :] = recv_ref[:, 0, rows : 2 * rows, :].reshape(seg_rows, width)
+    cat_v[comp_rows:, 0:width] = recv_ref[:, 0, 2 * rows : 3 * rows, :].reshape(seg_rows, width)
     merge_taps(fine_k, conv_k_ref, comp_ref.at[0], win_k, rows_f32)
     merge_taps(fine_v, conv_v_ref, comp_ref.at[1], win_v, rows_f32)
     comp_k, comp_v = comp_ref[0], comp_ref[1]
@@ -210,12 +212,12 @@
 
         @pl.when(lax.rem(g - at_ref[0] + seg_count, seg_count) == i)
         def _():
-            share_ref[0 : 2 * comp_rows, :] = comp_ref[...].reshape(2 * comp_rows, width)
+            share_ref[...] = comp_ref[...]
 
     b0, s1, memory_from = doc_bounds(starts_ref, g, seg_rows, comp_rows)
 
     def queries(p0):
-        return recv_ref[0, p0 // rows : (p0 + step) // rows, 0:rows, :].reshape(step, width)
+        return recv_ref[p0 // rows : (p0 + step) // rows, 0, 0:rows, :].reshape(step, width)
 
     def weighted(weights, values_and_ones):
         mix = matmul(weights.astype(bf16), values_and_ones)
@@ -223,6 +225,7 @@
 
     def attend(fine_from_s1):
         fine, recon = {}, {}
+        value_rows, key_rows = [], []
 
         def fine_scores(p0):
             return matmul_t(queries(p0), fine_k[...])
@@ -241,7 +244,6 @@
             return matmul_t(queries(p0), comp_k)
 
         def comp_part(p0, scores):
-            here = slice(p0, p0 + step)
             _, comp_exp = softmax_part(scores, rate)
             total = jnp.sum(comp_exp, axis=1, keepdims=True)
             weights = comp_exp.astype(bf16)
@@ -251,9 +253,9 @@
             out_grad = (-2.0 * differ / total).astype(bf16)
             inner = matmul_t(out_grad, comp_v)
             offset = jnp.sum(out_grad.astype(jnp.float32) * recon_comp, axis=1, keepdims=True)
-            comp_w[here, :] = weights
-            out_grads[here, :] = out_grad
-            score_grads[here, :] = (comp_exp * (inner - offset)).astype(bf16)
+            score_grad = (comp_exp * (inner - offset)).astype(bf16)
+            value_rows.append(t_matmul(weights, out_grad))
+            key_rows.append(t_matmul(score_grad, queries(p0)))
 
         def cat_scores(p0):
             scores = matmul_t(queries(p0), cat_k[0 : comp_rows + p0 + step, :])
@@ -278,12 +280,13 @@
             for p0 in range(0, seg_rows, step)
             for part in ((fine_scores, fine_part), (cat_scores, cat_part), (comp_scores, comp_part))
         ]
-        ahead = parts[0][1](parts[0][0])
+        asked = [ask(p0) for p0, ask, _ in parts[:AHEAD]]
         for i, (p0, _, finish) in enumerate(parts):
-            scores = ahead
-            if i + 1 < len(parts):
-                ahead = parts[i + 1][1](parts[i + 1][0])
-            finish(p0, scores)
+            if i + AHEAD < len(parts):
+                asked.append(parts[i + AHEAD][1](parts[i + AHEAD][0]))
+            finish(p0, asked.pop(0))
+        sums[0] += t_matmul(win_k[...], (sum(key_rows) * scale).astype(bf16))
+        sums[1] += t_matmul(win_v[...], sum(value_rows).astype(bf16))
 
     @pl.when(s1 <= 0)
     def _():
@@ -294,17 +297,11 @@
         attend(True)
 
     def copy_out(i):
-        return pltpu.make_async_copy(out_rows.at[i], out_ref.at[i, :, 0:rows, :], sems.at[i])
+        return pltpu.make_async_copy(out_rows.at[i], out_ref.at[:, i, 0:rows, :], sems.at[i])
 
     copy_out(g).start()
     cat_k[0:comp_rows, :] = comp_k
     cat_v[0:comp_rows, 0:width] = comp_v
-    q = recv_ref[0, :, 0:rows, :].reshape(seg_rows, width)
-    value_rows = t_matmul(comp_w[...], out_grads[...]).astype(bf16)
-    key_rows = (t_matmul(score_grads[...], q) * scale).astype(bf16)
-    sums[0] += t_matmul(win_k[...], key_rows)
-    sums[1] += t_matmul(win_v[...], value_rows)
-
     @pl.when(g == seg_count - 1)
     def _():
         left = losses[...]
@@ -319,15 +316,13 @@
             loss_rows[0, s] = tail
         copies = [
             pltpu.make_async_copy(
-                loss_rows.at[0], out_ref.at[i, :, rows : rows + spare, :], sems.at[seg_count + i]
+                loss_rows.at[0], out_ref.at[:, i, rows : rows + spare, :], sems.at[seg_count + i]
             )
             for i in range(seg_count)
         ]
         for copy in copies:
             copy.start()
-        grads = sums[...].astype(bf16).reshape(-1, width)
-        for share_ref in share_refs:
-            share_ref[2 * comp_rows :, :] = grads
+        grad_ref[...] = sums[...].astype(bf16)
         for i in range(seg_count):
             copy_out(i).wait()
         for copy in copies:
@@ -335,16 +330,17 @@
 
 
 def head(starts, at, recv, conv_keys, conv_values):
-    seg_count, seq_count, block, width = recv.shape
+    seq_count, seg_count, block, width = recv.shape
     rows = block * seg_count // (3 * seg_count + 2)
     share = rows // seg_count
     seg_rows = rows * seq_count
     comp_rows = seg_rows // RATE
-    step = math.gcd(seg_rows, 256)
+    step = math.gcd(seg_rows, STEP)
     bf16, f32 = jnp.bfloat16, jnp.float32
     shape = jax.ShapeDtypeStruct
-    spare = 16
-    share_shape = (2 * comp_rows + 2 * RATE * width, width)
+    spare = 8
+    comp_shape = (2, comp_rows, width)
+    grad_shape = (2, RATE * width, width)
     conv = pl.BlockSpec((1, RATE * width, width), lambda g, starts, at: (at[0], 0, 0))
 
     def body(starts_ref, at_ref, *refs):
@@ -353,16 +349,17 @@
     return pl.pallas_call(
         body,
         out_shape=(
-            shape((seg_count, seq_count, rows + spare, width), bf16),
-            *[shape(share_shape, bf16)] * seg_count,
+            shape((seq_count, seg_count, rows + spare, width), bf16),
+            shape(grad_shape, bf16),
+            *[shape(comp_shape, bf16)] * seg_count,
         ),
         grid_spec=pltpu.PrefetchScalarGridSpec(
             num_scalar_prefetch=2,
             grid=(seg_count,),
             in_specs=[
-                pl.BlockSpec((1, seq_count, 3 * rows, width), lambda g, starts, at: (g, 0, 0, 0)),
+                pl.BlockSpec((seq_count, 1, 3 * rows, width), lambda g, starts, at: (0, g, 0, 0)),
                 pl.BlockSpec(
-                    (seg_count, seq_count, 2 * share, width),
+                    (seq_count, seg_count, 2 * share, width),
                     lambda g, starts, at: (0, 0, 3 * rows // (2 * share), 0),
                 ),
                 conv,
@@ -370,7 +367,8 @@
             ],
             out_specs=(
                 pl.BlockSpec(memory_space=pl.ANY),
-                *[pl.BlockSpec(share_shape, lambda g, starts, at: (0, 0))] * seg_count,
+                pl.BlockSpec(grad_shape, lambda g, starts, at: (0, 0, 0)),
+                *[pl.BlockSpec(comp_shape, lambda g, starts, at: (0, 0, 0))] * seg_count,
             ),
             scratch_shapes=[
                 pltpu.VMEM((seg_count, seq_count, rows, width), bf16),
@@ -383,9 +381,6 @@
                 pltpu.VMEM((seg_rows, width), f32),
                 pltpu.VMEM((comp_rows, RATE * width), bf16),
                 pltpu.VMEM((comp_rows, RATE * width), bf16),
-                pltpu.VMEM((seg_rows, comp_rows), bf16),
-                pltpu.VMEM((seg_rows, width), bf16),
-                pltpu.VMEM((seg_rows, comp_rows), bf16),
                 pltpu.VMEM((2, RATE * width, width), f32),
                 pltpu.VMEM((1, width), f32),
                 pltpu.SemaphoreType.DMA((2 * seg_count,)),
@@ -400,33 +395,40 @@
 
 
 def share_kernel(at_ref, *refs):
-    shares, (comp_k_ref, comp_v_ref, grad_k_ref, grad_v_ref) = refs[:-4], refs[-4:]
-    heads, taps, width = grad_k_ref.shape
-    comp_rows = comp_k_ref.shape[0]
-    for step, ref in enumerate(shares):
+    arrived, (comp_k_ref, comp_v_ref, grad_k_ref, grad_v_ref) = refs[:-4], refs[-4:]
+    heads, _, width = grad_k_ref.shape
+    for step, ref in enumerate(arrived[:heads]):
         head_at = lax.rem(at_ref[0] - step + heads, heads)
         columns = pl.ds(pl.multiple_of(head_at * width, width), width)
-        comp_k_ref[:, columns] = ref[0:comp_rows, :]
-        comp_v_ref[:, columns] = ref[comp_rows : 2 * comp_rows, :]
-        grads = ref[2 * comp_rows :, :].astype(jnp.float32)
-        grad_k_ref[head_at] = grads[0:taps]
-        grad_v_ref[head_at] = grads[taps:]
-
-
-def shared(at, shares, comp_rows, taps):
-    heads = len(shares)
-    width = shares[0].shape[1]
-    arrived = [shares[0]]
+        comp_k_ref[:, columns] = ref[0]
+        comp_v_ref[:, columns] = ref[1]
+    for step, ref in enumerate(arrived[heads:]):
+        grads = ref[...].astype(jnp.float32)
+        grad_k_ref[at_ref[0] ^ step] = grads[0]
+        grad_v_ref[at_ref[0] ^ step] = grads[1]
+
+
+def shared(at, comps, grads):
+    heads = len(comps)
+    comp_rows, width = comps[0].shape[1:]
+    arrived = [comps[0]]
     for step in range(1, heads):
         route = [(i, (i + step) % heads) for i in range(heads)]
-        arrived.append(lax.ppermute(shares[step], "seg", route))
-    comp = jax.ShapeDtypeStruct((comp_rows, heads * width), shares[0].dtype)
-    grad = jax.ShapeDtypeStruct((heads, taps, width), jnp.float32)
+        arrived.append(lax.ppermute(comps[step], "seg", route))
+    held = {0: grads}
+    bit = heads // 2
+    while bit:
+        route = [(i, i ^ bit) for i in range(heads)]
+        held |= {k ^ bit: lax.ppermute(x, "seg", route) for k, x in held.items()}
+        bit //= 2
+    arrived += [held[k] for k in range(heads)]
+    comp = jax.ShapeDtypeStruct((comp_rows, heads * width), grads.dtype)
+    grad = jax.ShapeDtypeStruct((heads, *grads.shape[1:]), jnp.float32)
     in_vmem = pl.BlockSpec(memory_space=pltpu.VMEM)
     return pl.pallas_call(
         share_kernel,
         out_shape=(comp, comp, grad, grad),
-        in_specs=[pl.BlockSpec(memory_space=pltpu.SMEM), *[in_vmem] * heads],
+        in_specs=[pl.BlockSpec(memory_space=pltpu.SMEM), *[in_vmem] * len(arrived)],
         out_specs=(in_vmem,) * 4,
         compiler_params=on_vmem(12),
         name="shared",
@@ -449,11 +451,9 @@
         return flat.reshape(blocks.shape)
 
     packed = pack(at, (queries, keys, values), (prior_keys, prior_values), seg_count, seq_count)
-    attended, *shares = head(doc_starts, at, exchanged(packed), conv_keys, conv_values)
+    attended, grads, *comps = head(doc_starts, at, exchanged(packed), conv_keys, conv_values)
     attended, loss = unpack(exchanged(attended), rows, count * rows)
-    comp_keys, comp_values, grad_k, grad_v = shared(
-        at, shares, rows * seq_count // RATE, conv_keys.shape[1]
-    )
+    comp_keys, comp_values, grad_k, grad_v = shared(at, comps, grads)
     return (attended, comp_keys, comp_values, loss[0, 0], grad_k, grad_v)
 
 

time: 155 us -> 151 us (0.974)
  waiting for transfers between devices: 26.9 us -> 23.6 us
    ppermute x3 -> x6, waiting for transfers between devices: 26.9 us -> 23.6 us  [the longest x3 17.1 us: shared(): held |= {k ^ bit: lax.ppermute(x, 'seg', route) for k, x in held.items()}]
    ppermute x3 -> x6, starting transfers between devices: 3.15 us -> 3.7 us  [the longest x3 1.86 us: shared(): arrived.append(lax.ppermute(comps[step], 'seg', route))]
  transfers between devices with their start and end apart: 4 -> 7, of which waited for: 3 -> 3; matrix products, arithmetic and copies ran while one was open for 0% -> 0% of each run, Pallas kernels for 1% -> 1%
where the time goes in v3:
time: 151 us; the launch traced here: 149 us
  blocking collectives  90.3 us (60%)
  Pallas kernels  27.8 us (18%)
  waiting for transfers between devices  23.6 us (16%)
  starting transfers between devices  6.87 us (5%)
    all_to_all x1, blocking collectives, exchanged(): flat = lax.all_to_all(flat, BOTH, split_axis=0, concat_axis=0, tiled=True)  90.3 us
    pallas_call x1, Pallas kernels, head(): pl.pallas_call(body, out_shape=(shape((seq_count, seg_count, rows + spare...  20.4 us
    ppermute x3, waiting for transfers between devices, shared(): held |= {k ^ bit: lax.ppermute(x, 'seg', route) for k, x in held.items()}  17.1 us
    ppermute x3, waiting for transfers between devices, shared(): arrived.append(lax.ppermute(comps[step], 'seg', route))  6.52 us
    pallas_call x1, Pallas kernels, pack(): pl.pallas_call(pack_kernel, out_shape=jax.ShapeDtypeStruct((seq_count, se...  3.57 us
    all_to_all x1, starting transfers between devices, exchanged(): flat = lax.all_to_all(flat, BOTH, split_axis=0, concat_axis=0, tiled=True)  3.17 us
  transfers between devices with their start and end apart: 7, of which 3 were waited for; matrix products, arithmetic and copies ran while one was open for 0% of the time, Pallas kernels for 1%

profile of v3, /device:TPU:0, one launch (start us, length us, event | category | flops | bytes accessed | tf_op | source)
XLA Modules:
  0.0 149.3 jit_solution(1438432028122351040)
XLA Ops:
  0.6 3.6 %pack.1 = bf16[8,4,448,128]{3,2,1,0:T(8,128)(2,1)} custom-call(s32[1]{0:T(128)} %bitcast.at_ref, bf16[128,4096]{1,0:T(8,128)(2,1)} %refs_0_.1, bf16[128,4096]{1,0:T(8,128)(2,1)} %refs_1_.1, bf16[128,4096]{1,0:T(8,128)(2,1)} %refs_2_.2, bf16[128,4096]{1,0:T(8,128)(2,1)} %refs_3_.2, bf16[128,4096]{1,0:T(8,128)(2,1)} %refs_4_.1), custom_call_target="tpu_custom_call" | custom-call | tf_op jit(solution)/shard_map/pack/pallas_call | solution.py:43
  4.2 0.0 copy-start
  4.2 0.0 copy-start.1
  4.2 0.0 copy-start.2
  4.2 90.3 %all_to_all.10 = bf16[32,448,128]{2,1,0:T(8,128)(2,1)S(1)} all-to-all(bf16[32,448,128]{2,1,0:T(8,128)(2,1)} %bitcast.9), channel_id=1, replica_groups=mesh['seg'=4,'seq'=8] {'seq','seg'}, dimensions={0} | all-to-all | bytes 7340032 | tf_op jit(solution)/shard_map/all_to_all | solution.py:450
  94.5 0.0 copy-done
  94.5 0.0 copy-done.1
  94.5 0.0 copy-done.2
  94.5 20.4 %head.1 = (bf16[8,4,136,128]{3,2,1,0:T(8,128)(2,1)}, bf16[2,512,128]{2,1,0:T(8,128)(2,1)S(1)}, bf16[2,256,128]{2,1,0:T(8,128)(2,1)S(1)}, bf16[2,256,128]{2,1,0:T...) custom-call(s32[4]{0:T(128)S(1)} %copy-done.2, s32[1]{0:T(128)} %bitcast.at_ref, ...), custom_call_target="tpu_custom_call" | custom-call | flops 10737418240 | bytes 8388608 | tf_op jit(solution)/shard_map/head/pallas_call | solution.py:349
  115.0 3.2 %all-to-all-start.1 = ((bf16[32,136,128]{2,1,0:T(8,128)(2,1)}), bf16[32,136,128]{2,1,0:T(8,128)(2,1)S(1)}, u32[]{:S(2)}, u32[]{:S(2)}) async-start(bf16[32,136,128]{2,1,0:T(8,128)(2,1)} %bitcast.3), calls=%async_computation.1 | async-start | bytes 2228224 | tf_op jit(solution)/shard_map/all_to_all | solution.py:450
  118.1 1.8 %collective-permute-start.4 = (bf16[2,512,128]{2,1,0:T(8,128)(2,1)S(1)}, bf16[2,512,128]{2,1,0:T(8,128)(2,1)S(1)}, u32[]{:S(2)}, u32[]{:S(2)}) collective-permute-start(bf16[2,512,128]{2,1,0:T(8,128)(2,1)S(1)} %get-tuple-element.24.refs_4_), channel_id=1, source_target_pairs={{0,16},{8,24},{16,0},{24,8},{1,17},{9,25},{17,1},{25,9},{2,18},{10... | collective-permute-start | bytes 786440 | tf_op jit(solution)/shard_map/ppermute | solution.py:422
  120.0 0.0 collective-permute-start.3
  120.0 17.1 %collective-permute-done.4.refs_6_ = bf16[2,512,128]{2,1,0:T(8,128)(2,1)S(1)} collective-permute-done((bf16[2,512,128]{2,1,0:T(8,128)(2,1)S(1)}, bf16[2,512,128]{2,1,0:T(8,128)(2,1)S(1)}, u32[]{:S(2)}, u32[]{:S(2)}) %collective-permute-start.4) | collective-permute-done | bytes 262176 | tf_op jit(solution)/shard_map/ppermute | solution.py:422
  137.1 0.0 collective-permute-start.5
  137.1 0.5 collective-permute-start
  137.6 0.0 collective-permute-start.1
  137.6 1.4 collective-permute-start.2
  138.9 2.8 %collective-permute-done.refs_1_ = bf16[2,256,128]{2,1,0:T(8,128)(2,1)S(1)} collective-permute-done((bf16[2,256,128]{2,1,0:T(8,128)(2,1)S(1)}, bf16[2,256,128]{2,1,0:T(8,128)(2,1)S(1)}, u32[]{:S(2)}, u32[]{:S(2)}) %collective-permute-start) | collective-permute-done | bytes 131104 | tf_op jit(solution)/shard_map/ppermute | solution.py:417
  141.8 3.7 %collective-permute-done.1.refs_2_ = bf16[2,256,128]{2,1,0:T(8,128)(2,1)S(1)} collective-permute-done((bf16[2,256,128]{2,1,0:T(8,128)(2,1)S(1)}, bf16[2,256,128]{2,1,0:T(8,128)(2,1)S(1)}, u32[]{:S(2)}, u32[]{:S(2)}) %collective-permute-start.1) | collective-permute-done | bytes 131104 | tf_op jit(solution)/shard_map/ppermute | solution.py:417
  145.4 0.0 collective-permute-done.2.refs_3_
  145.4 0.0 collective-permute-done.3.refs_5_
  145.5 0.0 collective-permute-done.5.refs_7_
  145.5 1.7 %shared.1 = (bf16[256,512]{1,0:T(8,128)(2,1)}, bf16[256,512]{1,0:T(8,128)(2,1)}, f32[4,512,128]{2,1,0:T(8,128)}, f32[4,512,128]{2,1,0:T(8,128)}) custom-call(s32[1]{0:T(128)} %bitcast.at_ref, bf16[2,256,128]{2,1,0:T(8,128)(2,1)S(1)} %get-tuple-element.20.refs_0_, bf16[2,256,128]{2,1,0:T(8,128)(2,1)S(1)} %collective-permute-done.refs_1_, ...), custom_call_target="tpu_custom_call" | custom-call | tf_op jit(solution)/shard_map/shared/pallas_call | solution.py:428
  147.1 0.0 all-to-all-done.1
  147.1 2.1 %unpack.1 = (bf16[128,4096]{1,0:T(8,128)(2,1)}, f32[1,1]{1,0:T(1,128)}) custom-call(bf16[8,4,136,128]{3,2,1,0:T(8,128)(2,1)S(1)} %bitcast.6), custom_call_target="tpu_custom_call" | custom-call | tf_op jit(solution)/shard_map/unpack/pallas_call | solution.py:93
Async XLA Ops:
  4.2 90.3 %copy-start = (bf16[4,512,128]{2,1,0:T(8,128)(2,1)S(1)}, bf16[4,512,128]{2,1,0:T(8,128)(2,1)}, u32[]{:S(2)}) copy-start(bf16[4,512,128]{2,1,0:T(8,128)(2,1)} %refs_2_.3) | copy-start | bytes 1572868
  4.2 90.3 %copy-start.1 = (bf16[4,512,128]{2,1,0:T(8,128)(2,1)S(1)}, bf16[4,512,128]{2,1,0:T(8,128)(2,1)}, u32[]{:S(2)}) copy-start(bf16[4,512,128]{2,1,0:T(8,128)(2,1)} %refs_3_.3) | copy-start | bytes 1572868
  4.2 90.3 %copy-start.2 = (s32[4]{0:T(128)S(1)}, s32[4]{0:T(128)}, u32[]{:S(2)}) copy-start(s32[4]{0:T(128)} %starts_ref.1) | copy-start | bytes 52
  115.0 32.2 %all-to-all-start.1 = ((bf16[32,136,128]{2,1,0:T(8,128)(2,1)}), bf16[32,136,128]{2,1,0:T(8,128)(2,1)S(1)}, u32[]{:S(2)}, u32[]{:S(2)}) async-start(bf16[32,136,128]{2,1,0:T(8,128)(2,1)} %bitcast.3), calls=%async_computation.1 | async-start | bytes 2228224 | tf_op jit(solution)/shard_map/all_to_all | solution.py:450
  118.1 18.9 %collective-permute-start.4 = (bf16[2,512,128]{2,1,0:T(8,128)(2,1)S(1)}, bf16[2,512,128]{2,1,0:T(8,128)(2,1)S(1)}, u32[]{:S(2)}, u32[]{:S(2)}) collective-permute-start(bf16[2,512,128]{2,1,0:T(8,128)(2,1)S(1)} %get-tuple-element.24.refs_4_), channel_id=1, source_target_pairs={{0,16},{8,24},{16,0},{24,8},{1,17},{9,25},{17,1},{25,9},{2,18},{10... | collective-permute-start | bytes 786440 | tf_op jit(solution)/shard_map/ppermute | solution.py:422
  120.0 25.5 %collective-permute-start.3 = (bf16[2,512,128]{2,1,0:T(8,128)(2,1)S(1)}, bf16[2,512,128]{2,1,0:T(8,128)(2,1)S(1)}, u32[]{:S(2)}, u32[]{:S(2)}) collective-permute-start(bf16[2,512,128]{2,1,0:T(8,128)(2,1)S(1)} %get-tuple-element.24.refs_4_), channel_id=1, source_target_pairs={{0,8},{8,0},{16,24},{24,16},{1,9},{9,1},{17,25},{25,17},{2,10},{10... | collective-permute-start | bytes 786440 | tf_op jit(solution)/shard_map/ppermute | solution.py:422
  137.1 8.4 %collective-permute-start.5 = (bf16[2,512,128]{2,1,0:T(8,128)(2,1)S(1)}, bf16[2,512,128]{2,1,0:T(8,128)(2,1)S(1)}, u32[]{:S(2)}, u32[]{:S(2)}) collective-permute-start(bf16[2,512,128]{2,1,0:T(8,128)(2,1)S(1)} %collective-permute-done.4.refs_6_), channel_id=1, source_target_pairs={{0,8},{8,0},{16,24},{24,16},{1,9},{9,1},{17,25},{25,17},{2,10},{10... | collective-permute-start | bytes 786440 | tf_op jit(solution)/shard_map/ppermute | solution.py:422
  137.1 4.7 %collective-permute-start = (bf16[2,256,128]{2,1,0:T(8,128)(2,1)S(1)}, bf16[2,256,128]{2,1,0:T(8,128)(2,1)S(1)}, u32[]{:S(2)}, u32[]{:S(2)}) collective-permute-start(bf16[2,256,128]{2,1,0:T(8,128)(2,1)S(1)} %get-tuple-element.21), channel_id=1, source_target_pairs={{0,8},{8,16},{16,24},{24,0},{1,9},{9,17},{17,25},{25,1},{2,10},{10... | collective-permute-start | bytes 393224 | tf_op jit(solution)/shard_map/ppermute | solution.py:417
  137.6 7.9 %collective-permute-start.1 = (bf16[2,256,128]{2,1,0:T(8,128)(2,1)S(1)}, bf16[2,256,128]{2,1,0:T(8,128)(2,1)S(1)}, u32[]{:S(2)}, u32[]{:S(2)}) collective-permute-start(bf16[2,256,128]{2,1,0:T(8,128)(2,1)S(1)} %get-tuple-element.22), channel_id=1, source_target_pairs={{0,16},{8,24},{16,0},{24,8},{1,17},{9,25},{17,1},{25,9},{2,18},{10... | collective-permute-start | bytes 393224 | tf_op jit(solution)/shard_map/ppermute | solution.py:417
  137.6 7.9 %collective-permute-start.2 = (bf16[2,256,128]{2,1,0:T(8,128)(2,1)S(1)}, bf16[2,256,128]{2,1,0:T(8,128)(2,1)S(1)}, u32[]{:S(2)}, u32[]{:S(2)}) collective-permute-start(bf16[2,256,128]{2,1,0:T(8,128)(2,1)S(1)} %get-tuple-element.23), channel_id=1, source_target_pairs={{0,24},{8,0},{16,8},{24,16},{1,25},{9,1},{17,9},{25,17},{2,26},{10... | collective-permute-start | bytes 393224 | tf_op jit(solution)/shard_map/ppermute | solution.py:417

commit v4 on v3

--- a/solution.py
+++ b/solution.py
@@ -59,41 +59,35 @@
     )(at, *arrays, *prior_arrays)
 
 
-def unpack_kernel(positions, in_ref, out_ref, loss_ref, rows_ref, tails, sems):
+def unpack_kernel(positions, in_ref, out_ref, loss_ref, tails, sems):
     seq_count, seg_count, _, width = in_ref.shape
-    rows = rows_ref.shape[0]
+    rows = out_ref.shape[0]
+    spare = tails.shape[2]
+    count = seg_count * seq_count
+    tail = pltpu.make_async_copy(in_ref.at[:, :, rows : rows + spare, :], tails, sems.at[count])
+    tail.start()
     copies = []
-    for s in range(seq_count):
-        for r in range(seg_count):
-            at = s * seg_count + r
-            columns = slice(at * width, (at + 1) * width)
-            from_ref = in_ref.at[s, r, 0:rows, :]
-            copies.append(pltpu.make_async_copy(from_ref, rows_ref.at[:, columns], sems.at[at]))
-            copies[-1].start()
-    spare = tails.shape[2]
-    tail = pltpu.make_async_copy(
-        in_ref.at[:, :, rows : rows + spare, :], tails, sems.at[seg_count * seq_count]
-    )
-    tail.start()
-    for copy in copies:
-        copy.wait()
-    copy = pltpu.make_async_copy(rows_ref, out_ref, sems.at[seg_count * seq_count + 1])
-    copy.start()
+    for i in range(count):
+        from_ref = in_ref.at[i // seg_count, i % seg_count, 0:rows, :]
+        columns = slice(i * width, (i + 1) * width)
+        copies.append(pltpu.make_async_copy(from_ref, out_ref.at[:, columns], sems.at[i]))
+        copies[-1].start()
     tail.wait()
     parts = tails[...].reshape(-1, width).astype(jnp.float32)
     total = jnp.sum(jnp.sum(parts, axis=0, keepdims=True), axis=1, keepdims=True)
     loss_ref[...] = total / positions
-    copy.wait()
+    for copy in copies:
+        copy.wait()
 
 
 def unpack(blocks, rows, positions):
     seq_count, seg_count, _, width = blocks.shape
     spare = blocks.shape[2] - rows
-    shape = (rows, seg_count * seq_count * width)
+    count = seg_count * seq_count
     return pl.pallas_call(
         functools.partial(unpack_kernel, positions),
         out_shape=(
-            jax.ShapeDtypeStruct(shape, blocks.dtype),
+            jax.ShapeDtypeStruct((rows, count * width), blocks.dtype),
             jax.ShapeDtypeStruct((1, 1), jnp.float32),
         ),
         in_specs=[pl.BlockSpec(memory_space=pl.ANY)],
@@ -102,9 +96,8 @@
             pl.BlockSpec(memory_space=pltpu.VMEM),
         ),
         scratch_shapes=[
-            pltpu.VMEM(shape, blocks.dtype),
             pltpu.VMEM((seq_count, seg_count, spare, width), blocks.dtype),
-            pltpu.SemaphoreType.DMA((seg_count * seq_count + 2,)),
+            pltpu.SemaphoreType.DMA((count + 1,)),
         ],
         compiler_params=on_vmem(8),
         name="unpack",
@@ -419,7 +412,10 @@
     bit = heads // 2
     while bit:
         route = [(i, i ^ bit) for i in range(heads)]
-        held |= {k ^ bit: lax.ppermute(x, "seg", route) for k, x in held.items()}
+        came = [lax.ppermute(x, "seg", route) for x in held.values()]
+        if bit > 1:
+            came, arrived = lax.optimization_barrier((came, arrived))
+        held |= {k ^ bit: x for k, x in zip(held, came)}
         bit //= 2
     arrived += [held[k] for k in range(heads)]
     comp = jax.ShapeDtypeStruct((comp_rows, heads * width), grads.dtype)

time: 151 us -> 149 us (0.987)
  waiting for transfers between devices: 23.6 us -> 19.9 us
  starting transfers between devices: 6.87 us -> 10.1 us
    ppermute x3, waiting for transfers between devices: 17.1 us -> 1.16 us  [shared(): came = [lax.ppermute(x, 'seg', route) for x in held.values()]]
    ppermute x3, waiting for transfers between devices: 6.52 us -> 18.7 us  [shared(): arrived.append(lax.ppermute(comps[step], 'seg', route))]
    ppermute x3, starting transfers between devices: 1.84 us -> 5.1 us  [shared(): came = [lax.ppermute(x, 'seg', route) for x in held.values()]]
  transfers between devices with their start and end apart: 7 -> 7, of which waited for: 3 -> 4; matrix products, arithmetic and copies ran while one was open for 0% -> 0% of each run, Pallas kernels for 1% -> 1%
where the time goes in v4:
time: 149 us; the launch traced here: 148 us
  blocking collectives  90.3 us (61%)
  Pallas kernels  27.4 us (18%)
  waiting for transfers between devices  19.9 us (13%)
  starting transfers between devices  10.1 us (7%)
    all_to_all x1, blocking collectives, exchanged(): flat = lax.all_to_all(flat, BOTH, split_axis=0, concat_axis=0, tiled=True)  90.3 us
    pallas_call x1, Pallas kernels, head(): pl.pallas_call(body, out_shape=(shape((seq_count, seg_count, rows + spare...  20.4 us
    ppermute x3, waiting for transfers between devices, shared(): arrived.append(lax.ppermute(comps[step], 'seg', route))  18.7 us
    ppermute x3, starting transfers between devices, shared(): came = [lax.ppermute(x, 'seg', route) for x in held.values()]  5.1 us
    pallas_call x1, Pallas kernels, pack(): pl.pallas_call(pack_kernel, out_shape=jax.ShapeDtypeStruct((seq_count, se...  3.57 us
    all_to_all x1, starting transfers between devices, exchanged(): flat = lax.all_to_all(flat, BOTH, split_axis=0, concat_axis=0, tiled=True)  3.17 us
  transfers between devices with their start and end apart: 7, of which 4 were waited for; matrix products, arithmetic and copies ran while one was open for 0% of the time, Pallas kernels for 1%

profile of v4, /device:TPU:0, one launch (start us, length us, event | category | flops | bytes accessed | tf_op | source)
XLA Modules:
  0.0 148.3 jit_solution(2118483672999206520)
XLA Ops:
  0.6 3.6 %pack.1 = bf16[8,4,448,128]{3,2,1,0:T(8,128)(2,1)} custom-call(s32[1]{0:T(128)} %bitcast.at_ref, bf16[128,4096]{1,0:T(8,128)(2,1)} %refs_0_.1, bf16[128,4096]{1,0:T(8,128)(2,1)} %refs_1_.1, bf16[128,4096]{1,0:T(8,128)(2,1)} %refs_2_.2, bf16[128,4096]{1,0:T(8,128)(2,1)} %refs_3_.2, bf16[128,4096]{1,0:T(8,128)(2,1)} %refs_4_.1), custom_call_target="tpu_custom_call" | custom-call | tf_op jit(solution)/shard_map/pack/pallas_call | solution.py:43
  4.2 0.0 copy-start
  4.2 0.0 copy-start.1
  4.2 0.0 copy-start.2
  4.2 90.3 %all_to_all.10 = bf16[32,448,128]{2,1,0:T(8,128)(2,1)S(1)} all-to-all(bf16[32,448,128]{2,1,0:T(8,128)(2,1)} %bitcast.9), channel_id=1, replica_groups=mesh['seg'=4,'seq'=8] {'seq','seg'}, dimensions={0} | all-to-all | bytes 7340032 | tf_op jit(solution)/shard_map/all_to_all | solution.py:446
  94.5 0.0 copy-done
  94.5 0.0 copy-done.1
  94.5 0.0 copy-done.2
  94.5 20.4 %head.1 = (bf16[8,4,136,128]{3,2,1,0:T(8,128)(2,1)}, bf16[2,512,128]{2,1,0:T(8,128)(2,1)S(1)}, bf16[2,256,128]{2,1,0:T(8,128)(2,1)S(1)}, bf16[2,256,128]{2,1,0:T...) custom-call(s32[4]{0:T(128)S(1)} %copy-done.2, s32[1]{0:T(128)} %bitcast.at_ref, ...), custom_call_target="tpu_custom_call" | custom-call | flops 10737418240 | bytes 8388608 | tf_op jit(solution)/shard_map/head/pallas_call | solution.py:342
  115.0 3.2 %all-to-all-start.1 = ((bf16[32,136,128]{2,1,0:T(8,128)(2,1)}), bf16[32,136,128]{2,1,0:T(8,128)(2,1)S(1)}, u32[]{:S(2)}, u32[]{:S(2)}) async-start(bf16[32,136,128]{2,1,0:T(8,128)(2,1)} %bitcast.3), calls=%async_computation.1 | async-start | bytes 2228224 | tf_op jit(solution)/shard_map/all_to_all | solution.py:446
  118.1 1.8 %collective-permute-start = (bf16[2,512,128]{2,1,0:T(8,128)(2,1)S(1)}, bf16[2,512,128]{2,1,0:T(8,128)(2,1)S(1)}, u32[]{:S(2)}, u32[]{:S(2)}) collective-permute-start(bf16[2,512,128]{2,1,0:T(8,128)(2,1)S(1)} %get-tuple-element.25.refs_4_), channel_id=1, source_target_pairs={{0,16},{8,24},{16,0},{24,8},{1,17},{9,25},{17,1},{25,9},{2,18},{10... | collective-permute-start | bytes 786440 | tf_op jit(solution)/shard_map/ppermute | solution.py:415
  120.0 0.0 collective-permute-start.1
  120.0 0.3 collective-permute-start.2
  120.3 1.5 %collective-permute-start.3 = (bf16[2,256,128]{2,1,0:T(8,128)(2,1)S(1)}, bf16[2,256,128]{2,1,0:T(8,128)(2,1)S(1)}, u32[]{:S(2)}, u32[]{:S(2)}) collective-permute-start(bf16[2,256,128]{2,1,0:T(8,128)(2,1)S(1)} %get-tuple-element.29), channel_id=1, source_target_pairs={{0,24},{8,0},{16,8},{24,16},{1,25},{9,1},{17,9},{25,17},{2,26},{10... | collective-permute-start | bytes 393224 | tf_op jit(solution)/shard_map/ppermute | solution.py:410
  121.8 0.1 collective-permute-start.4
  121.8 17.5 %collective-permute-done.1.refs_1_ = bf16[2,256,128]{2,1,0:T(8,128)(2,1)S(1)} collective-permute-done((bf16[2,256,128]{2,1,0:T(8,128)(2,1)S(1)}, bf16[2,256,128]{2,1,0:T(8,128)(2,1)S(1)}, u32[]{:S(2)}, u32[]{:S(2)}) %collective-permute-start.1) | collective-permute-done | bytes 131104 | tf_op jit(solution)/shard_map/ppermute | solution.py:410
  139.4 1.0 collective-permute-done.2.refs_2_
  140.3 0.2 collective-permute-done.3.refs_3_
  140.6 0.0 collective-permute-done.refs_6_
  140.6 3.2 %collective-permute-start.5 = (bf16[2,512,128]{2,1,0:T(8,128)(2,1)S(1)}, bf16[2,512,128]{2,1,0:T(8,128)(2,1)S(1)}, u32[]{:S(2)}, u32[]{:S(2)}) collective-permute-start(bf16[2,512,128]{2,1,0:T(8,128)(2,1)S(1)} %collective-permute-done.refs_6_), channel_id=1, source_target_pairs={{0,8},{8,0},{16,24},{24,16},{1,9},{9,1},{17,25},{25,17},{2,10},{10... | collective-permute-start | bytes 786440 | tf_op jit(solution)/shard_map/ppermute | solution.py:415
  143.7 0.0 collective-permute-done.4.refs_5_
  143.7 1.2 collective-permute-done.5.refs_7_
  144.9 1.7 %shared.1 = (bf16[256,512]{1,0:T(8,128)(2,1)}, bf16[256,512]{1,0:T(8,128)(2,1)}, f32[4,512,128]{2,1,0:T(8,128)}, f32[4,512,128]{2,1,0:T(8,128)}) custom-call(s32[1]{0:T(128)} %bitcast.at_ref, bf16[2,256,128]{2,1,0:T(8,128)(2,1)S(1)} %get-tuple-element.30.refs_0_, bf16[2,256,128]{2,1,0:T(8,128)(2,1)S(1)} %collective-permute-done.1.refs_1_, ...), custom_call_target="tpu_custom_call" | custom-call | tf_op jit(solution)/shard_map/shared/pallas_call | solution.py:424
  146.6 0.0 all-to-all-done.1
  146.6 1.8 %unpack.1 = (bf16[128,4096]{1,0:T(8,128)(2,1)}, f32[1,1]{1,0:T(1,128)}) custom-call(bf16[8,4,136,128]{3,2,1,0:T(8,128)(2,1)S(1)} %bitcast.6), custom_call_target="tpu_custom_call" | custom-call | tf_op jit(solution)/shard_map/unpack/pallas_call | solution.py:87
Async XLA Ops:
  4.2 90.3 %copy-start = (bf16[4,512,128]{2,1,0:T(8,128)(2,1)S(1)}, bf16[4,512,128]{2,1,0:T(8,128)(2,1)}, u32[]{:S(2)}) copy-start(bf16[4,512,128]{2,1,0:T(8,128)(2,1)} %refs_2_.3) | copy-start | bytes 1572868
  4.2 90.3 %copy-start.1 = (bf16[4,512,128]{2,1,0:T(8,128)(2,1)S(1)}, bf16[4,512,128]{2,1,0:T(8,128)(2,1)}, u32[]{:S(2)}) copy-start(bf16[4,512,128]{2,1,0:T(8,128)(2,1)} %refs_3_.3) | copy-start | bytes 1572868
  4.2 90.3 %copy-start.2 = (s32[4]{0:T(128)S(1)}, s32[4]{0:T(128)}, u32[]{:S(2)}) copy-start(s32[4]{0:T(128)} %starts_ref.1) | copy-start | bytes 52
  115.0 31.6 %all-to-all-start.1 = ((bf16[32,136,128]{2,1,0:T(8,128)(2,1)}), bf16[32,136,128]{2,1,0:T(8,128)(2,1)S(1)}, u32[]{:S(2)}, u32[]{:S(2)}) async-start(bf16[32,136,128]{2,1,0:T(8,128)(2,1)} %bitcast.3), calls=%async_computation.1 | async-start | bytes 2228224 | tf_op jit(solution)/shard_map/all_to_all | solution.py:446
  118.1 22.4 %collective-permute-start = (bf16[2,512,128]{2,1,0:T(8,128)(2,1)S(1)}, bf16[2,512,128]{2,1,0:T(8,128)(2,1)S(1)}, u32[]{:S(2)}, u32[]{:S(2)}) collective-permute-start(bf16[2,512,128]{2,1,0:T(8,128)(2,1)S(1)} %get-tuple-element.25.refs_4_), channel_id=1, source_target_pairs={{0,16},{8,24},{16,0},{24,8},{1,17},{9,25},{17,1},{25,9},{2,18},{10... | collective-permute-start | bytes 786440 | tf_op jit(solution)/shard_map/ppermute | solution.py:415
  120.0 19.4 %collective-permute-start.1 = (bf16[2,256,128]{2,1,0:T(8,128)(2,1)S(1)}, bf16[2,256,128]{2,1,0:T(8,128)(2,1)S(1)}, u32[]{:S(2)}, u32[]{:S(2)}) collective-permute-start(bf16[2,256,128]{2,1,0:T(8,128)(2,1)S(1)} %get-tuple-element.27), channel_id=1, source_target_pairs={{0,8},{8,16},{16,24},{24,0},{1,9},{9,17},{17,25},{25,1},{2,10},{10... | collective-permute-start | bytes 393224 | tf_op jit(solution)/shard_map/ppermute | solution.py:410
  120.0 20.4 %collective-permute-start.2 = (bf16[2,256,128]{2,1,0:T(8,128)(2,1)S(1)}, bf16[2,256,128]{2,1,0:T(8,128)(2,1)S(1)}, u32[]{:S(2)}, u32[]{:S(2)}) collective-permute-start(bf16[2,256,128]{2,1,0:T(8,128)(2,1)S(1)} %get-tuple-element.28), channel_id=1, source_target_pairs={{0,16},{8,24},{16,0},{24,8},{1,17},{9,25},{17,1},{25,9},{2,18},{10... | collective-permute-start | bytes 393224 | tf_op jit(solution)/shard_map/ppermute | solution.py:410
  120.3 20.3 %collective-permute-start.3 = (bf16[2,256,128]{2,1,0:T(8,128)(2,1)S(1)}, bf16[2,256,128]{2,1,0:T(8,128)(2,1)S(1)}, u32[]{:S(2)}, u32[]{:S(2)}) collective-permute-start(bf16[2,256,128]{2,1,0:T(8,128)(2,1)S(1)} %get-tuple-element.29), channel_id=1, source_target_pairs={{0,24},{8,0},{16,8},{24,16},{1,25},{9,1},{17,9},{25,17},{2,26},{10... | collective-permute-start | bytes 393224 | tf_op jit(solution)/shard_map/ppermute | solution.py:410
  121.8 22.0 %collective-permute-start.4 = (bf16[2,512,128]{2,1,0:T(8,128)(2,1)S(1)}, bf16[2,512,128]{2,1,0:T(8,128)(2,1)S(1)}, u32[]{:S(2)}, u32[]{:S(2)}) collective-permute-start(bf16[2,512,128]{2,1,0:T(8,128)(2,1)S(1)} %get-tuple-element.25.refs_4_), channel_id=1, source_target_pairs={{0,8},{8,0},{16,24},{24,16},{1,9},{9,1},{17,25},{25,17},{2,10},{10... | collective-permute-start | bytes 786440 | tf_op jit(solution)/shard_map/ppermute | solution.py:415
  140.6 4.3 %collective-permute-start.5 = (bf16[2,512,128]{2,1,0:T(8,128)(2,1)S(1)}, bf16[2,512,128]{2,1,0:T(8,128)(2,1)S(1)}, u32[]{:S(2)}, u32[]{:S(2)}) collective-permute-start(bf16[2,512,128]{2,1,0:T(8,128)(2,1)S(1)} %collective-permute-done.refs_6_), channel_id=1, source_target_pairs={{0,8},{8,0},{16,24},{24,16},{1,9},{9,1},{17,25},{25,17},{2,10},{10... | collective-permute-start | bytes 786440 | tf_op jit(solution)/shard_map/ppermute | solution.py:415

commit v5 on v4

--- a/solution.py
+++ b/solution.py
@@ -209,8 +209,10 @@
 
     b0, s1, memory_from = doc_bounds(starts_ref, g, seg_rows, comp_rows)
 
-    def queries(p0):
-        return recv_ref[p0 // rows : (p0 + step) // rows, 0, 0:rows, :].reshape(step, width)
+    def queries(p0, size=step):
+        return recv_ref[p0 // rows : (p0 + size) // rows, 0, 0:rows, :].reshape(size, width)
+
+    half = max(step // 2, rows)
 
     def weighted(weights, values_and_ones):
         mix = matmul(weights.astype(bf16), values_and_ones)
@@ -251,27 +253,32 @@
             key_rows.append(t_matmul(score_grad, queries(p0)))
 
         def cat_scores(p0):
-            scores = matmul_t(queries(p0), cat_k[0 : comp_rows + p0 + step, :])
+            scores = matmul_t(queries(p0, half), cat_k[0 : comp_rows + p0 + half, :])
             memory = memory_scores(scores[:, 0:comp_rows], p0, b0, memory_from)
             return jnp.concatenate((memory, own_scores(scores[:, comp_rows:], p0, b0)), axis=1)
 
         def cat_part(p0, scores):
             top, weights = softmax_part(scores, rate)
-            mix, total = weighted(weights, cat_v[0 : comp_rows + p0 + step, :])
-            fine_top, fine_mix, fine_total = fine.pop(p0)
-            seen = before_doc(step, p0, b0)
+            mix, total = weighted(weights, cat_v[0 : comp_rows + p0 + half, :])
+            at = p0 % step
+            fine_top, fine_mix, fine_total = (x[at : at + half] for x in fine[p0 - at])
+            seen = before_doc(half, p0, b0)
             both = jnp.where(seen, jnp.maximum(top, fine_top), top)
             fine_share = jnp.where(seen, jnp.exp2((fine_top - both) * rate), 0.0)
             cat_share = jnp.exp2((top - both) * rate)
             mix = mix * cat_share + fine_mix * fine_share
             total = total * cat_share + fine_total * fine_share
-            here = slice(p0 // rows, (p0 + step) // rows)
-            out_rows[g, here] = (mix / total).astype(bf16).reshape(step // rows, rows, width)
+            here = slice(p0 // rows, (p0 + half) // rows)
+            out_rows[g, here] = (mix / total).astype(bf16).reshape(half // rows, rows, width)
 
         parts = [
-            (p0, *part)
+            part
             for p0 in range(0, seg_rows, step)
-            for part in ((fine_scores, fine_part), (cat_scores, cat_part), (comp_scores, comp_part))
+            for part in (
+                (p0, fine_scores, fine_part),
+                *[(p, cat_scores, cat_part) for p in range(p0, p0 + step, half)],
+                (p0, comp_scores, comp_part),
+            )
         ]
         asked = [ask(p0) for p0, ask, _ in parts[:AHEAD]]
         for i, (p0, _, finish) in enumerate(parts):

time: 149 us -> 149 us (level)
  no operation moved by 1% of the time
where the time goes in v5:
time: 149 us; the launch traced here: 148 us
  blocking collectives  90.3 us (61%)
  Pallas kernels  27.4 us (18%)
  waiting for transfers between devices  19.9 us (13%)
  starting transfers between devices  10.1 us (7%)
    all_to_all x1, blocking collectives, exchanged(): flat = lax.all_to_all(flat, BOTH, split_axis=0, concat_axis=0, tiled=True)  90.3 us
    pallas_call x1, Pallas kernels, head(): pl.pallas_call(body, out_shape=(shape((seq_count, seg_count, rows + spare...  20.4 us
    ppermute x3, waiting for transfers between devices, shared(): arrived.append(lax.ppermute(comps[step], 'seg', route))  18.7 us
    ppermute x3, starting transfers between devices, shared(): came = [lax.ppermute(x, 'seg', route) for x in held.values()]  5.1 us
    pallas_call x1, Pallas kernels, pack(): pl.pallas_call(pack_kernel, out_shape=jax.ShapeDtypeStruct((seq_count, se...  3.57 us
    all_to_all x1, starting transfers between devices, exchanged(): flat = lax.all_to_all(flat, BOTH, split_axis=0, concat_axis=0, tiled=True)  3.17 us
  transfers between devices with their start and end apart: 7, of which 4 were waited for; matrix products, arithmetic and copies ran while one was open for 0% of the time, Pallas kernels for 1%

profile of v5, /device:TPU:0, one launch (start us, length us, event | category | flops | bytes accessed | tf_op | source)
XLA Modules:
  0.0 148.3 jit_solution(3792586062733790718)
XLA Ops:
  0.6 3.6 %pack.1 = bf16[8,4,448,128]{3,2,1,0:T(8,128)(2,1)} custom-call(s32[1]{0:T(128)} %bitcast.at_ref, bf16[128,4096]{1,0:T(8,128)(2,1)} %refs_0_.1, bf16[128,4096]{1,0:T(8,128)(2,1)} %refs_1_.1, bf16[128,4096]{1,0:T(8,128)(2,1)} %refs_2_.2, bf16[128,4096]{1,0:T(8,128)(2,1)} %refs_3_.2, bf16[128,4096]{1,0:T(8,128)(2,1)} %refs_4_.1), custom_call_target="tpu_custom_call" | custom-call | tf_op jit(solution)/shard_map/pack/pallas_call | solution.py:43
  4.2 0.0 copy-start
  4.2 0.0 copy-start.1
  4.2 0.0 copy-start.2
  4.2 90.3 %all_to_all.10 = bf16[32,448,128]{2,1,0:T(8,128)(2,1)S(1)} all-to-all(bf16[32,448,128]{2,1,0:T(8,128)(2,1)} %bitcast.9), channel_id=1, replica_groups=mesh['seg'=4,'seq'=8] {'seq','seg'}, dimensions={0} | all-to-all | bytes 7340032 | tf_op jit(solution)/shard_map/all_to_all | solution.py:453
  94.5 0.0 copy-done
  94.5 0.0 copy-done.1
  94.5 0.0 copy-done.2
  94.5 20.4 %head.1 = (bf16[8,4,136,128]{3,2,1,0:T(8,128)(2,1)}, bf16[2,512,128]{2,1,0:T(8,128)(2,1)S(1)}, bf16[2,256,128]{2,1,0:T(8,128)(2,1)S(1)}, bf16[2,256,128]{2,1,0:T...) custom-call(s32[4]{0:T(128)S(1)} %copy-done.2, s32[1]{0:T(128)} %bitcast.at_ref, ...), custom_call_target="tpu_custom_call" | custom-call | flops 10737418240 | bytes 8388608 | tf_op jit(solution)/shard_map/head/pallas_call | solution.py:349
  114.9 3.2 %all-to-all-start.1 = ((bf16[32,136,128]{2,1,0:T(8,128)(2,1)}), bf16[32,136,128]{2,1,0:T(8,128)(2,1)S(1)}, u32[]{:S(2)}, u32[]{:S(2)}) async-start(bf16[32,136,128]{2,1,0:T(8,128)(2,1)} %bitcast.3), calls=%async_computation.1 | async-start | bytes 2228224 | tf_op jit(solution)/shard_map/all_to_all | solution.py:453
  118.1 1.8 %collective-permute-start = (bf16[2,512,128]{2,1,0:T(8,128)(2,1)S(1)}, bf16[2,512,128]{2,1,0:T(8,128)(2,1)S(1)}, u32[]{:S(2)}, u32[]{:S(2)}) collective-permute-start(bf16[2,512,128]{2,1,0:T(8,128)(2,1)S(1)} %get-tuple-element.25.refs_4_), channel_id=1, source_target_pairs={{0,16},{8,24},{16,0},{24,8},{1,17},{9,25},{17,1},{25,9},{2,18},{10... | collective-permute-start | bytes 786440 | tf_op jit(solution)/shard_map/ppermute | solution.py:422
  119.9 0.0 collective-permute-start.1
  119.9 0.3 collective-permute-start.2
  120.2 1.5 %collective-permute-start.3 = (bf16[2,256,128]{2,1,0:T(8,128)(2,1)S(1)}, bf16[2,256,128]{2,1,0:T(8,128)(2,1)S(1)}, u32[]{:S(2)}, u32[]{:S(2)}) collective-permute-start(bf16[2,256,128]{2,1,0:T(8,128)(2,1)S(1)} %get-tuple-element.29), channel_id=1, source_target_pairs={{0,24},{8,0},{16,8},{24,16},{1,25},{9,1},{17,9},{25,17},{2,26},{10... | collective-permute-start | bytes 393224 | tf_op jit(solution)/shard_map/ppermute | solution.py:417
  121.7 0.1 collective-permute-start.4
  121.8 17.5 %collective-permute-done.1.refs_1_ = bf16[2,256,128]{2,1,0:T(8,128)(2,1)S(1)} collective-permute-done((bf16[2,256,128]{2,1,0:T(8,128)(2,1)S(1)}, bf16[2,256,128]{2,1,0:T(8,128)(2,1)S(1)}, u32[]{:S(2)}, u32[]{:S(2)}) %collective-permute-start.1) | collective-permute-done | bytes 131104 | tf_op jit(solution)/shard_map/ppermute | solution.py:417
  139.3 1.0 collective-permute-done.2.refs_2_
  140.3 0.2 collective-permute-done.3.refs_3_
  140.5 0.0 collective-permute-done.refs_6_
  140.5 3.2 %collective-permute-start.5 = (bf16[2,512,128]{2,1,0:T(8,128)(2,1)S(1)}, bf16[2,512,128]{2,1,0:T(8,128)(2,1)S(1)}, u32[]{:S(2)}, u32[]{:S(2)}) collective-permute-start(bf16[2,512,128]{2,1,0:T(8,128)(2,1)S(1)} %collective-permute-done.refs_6_), channel_id=1, source_target_pairs={{0,8},{8,0},{16,24},{24,16},{1,9},{9,1},{17,25},{25,17},{2,10},{10... | collective-permute-start | bytes 786440 | tf_op jit(solution)/shard_map/ppermute | solution.py:422
  143.7 0.0 collective-permute-done.4.refs_5_
  143.7 1.2 collective-permute-done.5.refs_7_
  144.8 1.7 %shared.1 = (bf16[256,512]{1,0:T(8,128)(2,1)}, bf16[256,512]{1,0:T(8,128)(2,1)}, f32[4,512,128]{2,1,0:T(8,128)}, f32[4,512,128]{2,1,0:T(8,128)}) custom-call(s32[1]{0:T(128)} %bitcast.at_ref, bf16[2,256,128]{2,1,0:T(8,128)(2,1)S(1)} %get-tuple-element.30.refs_0_, bf16[2,256,128]{2,1,0:T(8,128)(2,1)S(1)} %collective-permute-done.1.refs_1_, ...), custom_call_target="tpu_custom_call" | custom-call | tf_op jit(solution)/shard_map/shared/pallas_call | solution.py:431
  146.5 0.0 all-to-all-done.1
  146.5 1.8 %unpack.1 = (bf16[128,4096]{1,0:T(8,128)(2,1)}, f32[1,1]{1,0:T(1,128)}) custom-call(bf16[8,4,136,128]{3,2,1,0:T(8,128)(2,1)S(1)} %bitcast.6), custom_call_target="tpu_custom_call" | custom-call | tf_op jit(solution)/shard_map/unpack/pallas_call | solution.py:87
Async XLA Ops:
  4.2 90.3 %copy-start = (bf16[4,512,128]{2,1,0:T(8,128)(2,1)S(1)}, bf16[4,512,128]{2,1,0:T(8,128)(2,1)}, u32[]{:S(2)}) copy-start(bf16[4,512,128]{2,1,0:T(8,128)(2,1)} %refs_2_.3) | copy-start | bytes 1572868
  4.2 90.3 %copy-start.1 = (bf16[4,512,128]{2,1,0:T(8,128)(2,1)S(1)}, bf16[4,512,128]{2,1,0:T(8,128)(2,1)}, u32[]{:S(2)}) copy-start(bf16[4,512,128]{2,1,0:T(8,128)(2,1)} %refs_3_.3) | copy-start | bytes 1572868
  4.2 90.3 %copy-start.2 = (s32[4]{0:T(128)S(1)}, s32[4]{0:T(128)}, u32[]{:S(2)}) copy-start(s32[4]{0:T(128)} %starts_ref.1) | copy-start | bytes 52
  114.9 31.6 %all-to-all-start.1 = ((bf16[32,136,128]{2,1,0:T(8,128)(2,1)}), bf16[32,136,128]{2,1,0:T(8,128)(2,1)S(1)}, u32[]{:S(2)}, u32[]{:S(2)}) async-start(bf16[32,136,128]{2,1,0:T(8,128)(2,1)} %bitcast.3), calls=%async_computation.1 | async-start | bytes 2228224 | tf_op jit(solution)/shard_map/all_to_all | solution.py:453
  118.1 22.4 %collective-permute-start = (bf16[2,512,128]{2,1,0:T(8,128)(2,1)S(1)}, bf16[2,512,128]{2,1,0:T(8,128)(2,1)S(1)}, u32[]{:S(2)}, u32[]{:S(2)}) collective-permute-start(bf16[2,512,128]{2,1,0:T(8,128)(2,1)S(1)} %get-tuple-element.25.refs_4_), channel_id=1, source_target_pairs={{0,16},{8,24},{16,0},{24,8},{1,17},{9,25},{17,1},{25,9},{2,18},{10... | collective-permute-start | bytes 786440 | tf_op jit(solution)/shard_map/ppermute | solution.py:422
  119.9 19.4 %collective-permute-start.1 = (bf16[2,256,128]{2,1,0:T(8,128)(2,1)S(1)}, bf16[2,256,128]{2,1,0:T(8,128)(2,1)S(1)}, u32[]{:S(2)}, u32[]{:S(2)}) collective-permute-start(bf16[2,256,128]{2,1,0:T(8,128)(2,1)S(1)} %get-tuple-element.27), channel_id=1, source_target_pairs={{0,8},{8,16},{16,24},{24,0},{1,9},{9,17},{17,25},{25,1},{2,10},{10... | collective-permute-start | bytes 393224 | tf_op jit(solution)/shard_map/ppermute | solution.py:417
  119.9 20.4 %collective-permute-start.2 = (bf16[2,256,128]{2,1,0:T(8,128)(2,1)S(1)}, bf16[2,256,128]{2,1,0:T(8,128)(2,1)S(1)}, u32[]{:S(2)}, u32[]{:S(2)}) collective-permute-start(bf16[2,256,128]{2,1,0:T(8,128)(2,1)S(1)} %get-tuple-element.28), channel_id=1, source_target_pairs={{0,16},{8,24},{16,0},{24,8},{1,17},{9,25},{17,1},{25,9},{2,18},{10... | collective-permute-start | bytes 393224 | tf_op jit(solution)/shard_map/ppermute | solution.py:417
  120.2 20.3 %collective-permute-start.3 = (bf16[2,256,128]{2,1,0:T(8,128)(2,1)S(1)}, bf16[2,256,128]{2,1,0:T(8,128)(2,1)S(1)}, u32[]{:S(2)}, u32[]{:S(2)}) collective-permute-start(bf16[2,256,128]{2,1,0:T(8,128)(2,1)S(1)} %get-tuple-element.29), channel_id=1, source_target_pairs={{0,24},{8,0},{16,8},{24,16},{1,25},{9,1},{17,9},{25,17},{2,26},{10... | collective-permute-start | bytes 393224 | tf_op jit(solution)/shard_map/ppermute | solution.py:417
  121.7 22.0 %collective-permute-start.4 = (bf16[2,512,128]{2,1,0:T(8,128)(2,1)S(1)}, bf16[2,512,128]{2,1,0:T(8,128)(2,1)S(1)}, u32[]{:S(2)}, u32[]{:S(2)}) collective-permute-start(bf16[2,512,128]{2,1,0:T(8,128)(2,1)S(1)} %get-tuple-element.25.refs_4_), channel_id=1, source_target_pairs={{0,8},{8,0},{16,24},{24,16},{1,9},{9,1},{17,25},{25,17},{2,10},{10... | collective-permute-start | bytes 786440 | tf_op jit(solution)/shard_map/ppermute | solution.py:422
  140.5 4.3 %collective-permute-start.5 = (bf16[2,512,128]{2,1,0:T(8,128)(2,1)S(1)}, bf16[2,512,128]{2,1,0:T(8,128)(2,1)S(1)}, u32[]{:S(2)}, u32[]{:S(2)}) collective-permute-start(bf16[2,512,128]{2,1,0:T(8,128)(2,1)S(1)} %collective-permute-done.refs_6_), channel_id=1, source_target_pairs={{0,8},{8,0},{16,24},{24,16},{1,9},{9,1},{17,25},{25,17},{2,10},{10... | collective-permute-start | bytes 786440 | tf_op jit(solution)/shard_map/ppermute | solution.py:422
